TPU v7x, 128 devices: a whole 4x4x4 slice. The times are simulated.
128 devices in a mesh: az: 16 (over x, y_lo, core), ax: 8 (over y_hi, z).
Axes of the slice: x: 4, y: 4 (y_hi: 2, y_lo: 2; y = y_hi * 2 + y_lo), z: 4, core: 2. Of those that a mesh axis runs over, the one named last changes fastest.
Arguments:
- fields: float32 [3, 64, 1024, 512], P(None, 'ax', 'az'), may hold values from -4.5 to 4.5
- conduct: float32 [1024, 512], P('az'), may hold values from 6000 to 24001
- kernel: float32 [128, 1024], P('ax', 'az'), may hold values from -0.1875 to 0.1875
Outputs:
- section: float32 [3, 64, 1024, 512], P(None, 'ax', 'az')
All inputs are finite; a program needn't handle non-finite values.
Results may differ from a plain program's by a relative error of at most 0.00035.
Values sent between devices are 32-bit elements; how exact they have to be, the bound alone decides.
A program may use at most 128 MiB of HBM per device.

v0:
```python
import math

import jax
import jax.numpy as jnp
from jax import lax
from jax.sharding import PartitionSpec as P

NEAR = 128


def shifted(block, axis, distance):
    devices = range(lax.axis_size(axis))
    route = [((i - distance) % len(devices), i) for i in devices]
    return lax.ppermute(block, axis, route)


def toeplitz_rows(window, rows, cols):
    length = rows + cols - 1
    flipped = jnp.flip(window, axis=-1)
    tiled = jnp.tile(flipped, (1, rows + 1))[:, : rows * (length + 1)]
    sliding = tiled.reshape(window.shape[0], rows, length + 1)[:, :, :cols]
    return jnp.flip(sliding, axis=1)


def shifted_back(values, stride, fill):
    padding = jnp.full((stride,) + values.shape[1:], fill, values.dtype)
    return jnp.concatenate([padding, values[:-stride]], axis=0)


def shifted_ahead(values, stride, fill):
    padding = jnp.full((stride,) + values.shape[1:], fill, values.dtype)
    return jnp.concatenate([values[stride:], padding], axis=0)


def cyclic_reduce(lower_diag, main_diag, upper_diag, system):
    count = main_diag.shape[0]
    padded_count = 1 << max(0, (count - 1).bit_length())
    extra = padded_count - count
    lower_diag = lower_diag.at[0].set(0.0)
    upper_diag = upper_diag.at[count - 1].set(0.0)
    zero_rows = jnp.zeros((extra,) + main_diag.shape[1:], jnp.float32)
    lower_diag = jnp.concatenate([lower_diag, zero_rows], axis=0)
    upper_diag = jnp.concatenate([upper_diag, zero_rows], axis=0)
    main_diag = jnp.concatenate([main_diag, zero_rows + 1.0], axis=0)
    system = jnp.concatenate([system, jnp.zeros((extra,) + system.shape[1:], jnp.float32)], axis=0)
    stride = 1
    while stride < padded_count:
        alpha = -lower_diag / shifted_back(main_diag, stride, 1.0)
        gamma = -upper_diag / shifted_ahead(main_diag, stride, 1.0)
        new_main = (
            main_diag
            + alpha * shifted_back(upper_diag, stride, 0.0)
            + gamma * shifted_ahead(lower_diag, stride, 0.0)
        )
        system = (
            system
            + alpha[:, None, :] * shifted_back(system, stride, 0.0)
            + gamma[:, None, :] * shifted_ahead(system, stride, 0.0)
        )
        lower_diag = alpha * shifted_back(lower_diag, stride, 0.0)
        upper_diag = gamma * shifted_ahead(upper_diag, stride, 0.0)
        main_diag = new_main
        stride = stride * 2
    return (system / main_diag[:, None, :])[:count]


def eliminate(sep_coefs, sep_rhs, behind, onward):
    behind_coefs, behind_rhs = behind
    onward_coefs, onward_rhs = onward
    weight_low = sep_coefs[..., 0, :] / behind_coefs[..., 1, :]
    weight_high = sep_coefs[..., 2, :] / onward_coefs[..., 1, :]
    coef_low = -weight_low * behind_coefs[..., 0, :]
    coef_high = -weight_high * onward_coefs[..., 2, :]
    coef_main = (
        sep_coefs[..., 1, :]
        - weight_low * behind_coefs[..., 2, :]
        - weight_high * onward_coefs[..., 0, :]
    )
    new_rhs = (
        sep_rhs
        - weight_low[..., None, None, :] * behind_rhs
        - weight_high[..., None, None, :] * onward_rhs
    )
    return (jnp.stack([coef_low, coef_main, coef_high], axis=-2), new_rhs)


def body(fields, conduct, kernel):
    cycle_count = lax.axis_size("az")
    position = lax.axis_index("az")
    field_count, planes, local_az, radial = fields.shape
    full_az = local_az * cycle_count
    gathered_cycles = lax.all_gather(kernel, "ax", axis=0, tiled=True)
    kernel_table = lax.all_gather(gathered_cycles, "az", axis=1, tiled=True)
    doubled_table = jnp.concatenate([kernel_table, kernel_table], axis=1)
    near_cycles = fields[..., :NEAR]
    cycle_group = math.gcd(NEAR, 32)
    groups = NEAR // cycle_group
    table_groups = doubled_table.reshape(groups, cycle_group, 2 * full_az)
    out_first = position * local_az
    shard_piece = lax.all_gather(near_cycles, "az", axis=2, tiled=True)
    length = shard_piece.shape[2]
    window_start = full_az + out_first - (length - 1)
    piece_groups = jnp.moveaxis(
        shard_piece.reshape(field_count, planes, length, groups, cycle_group), 3, 0
    )

    def one_group(paired):
        table_part, piece_part = paired
        window = lax.dynamic_slice_in_dim(table_part, window_start, local_az + length - 1, 1)
        circulant = toeplitz_rows(window, local_az, length)
        return jnp.einsum("ijk,fxki->fxji", circulant, piece_part, precision=lax.Precision.HIGHEST)

    mapped = lax.map(one_group, (table_groups, piece_groups))
    filtered = jnp.moveaxis(mapped, 0, 3).reshape(field_count, planes, local_az, NEAR)
    right_side = jnp.concatenate([filtered, fields[..., NEAR:]], axis=3)
    inner_count = local_az - 1
    columns = field_count * planes
    lower_diag = -conduct[:-1]
    upper_diag = -conduct[1:]
    main_diag = 1.0 + conduct[:-1] + conduct[1:]
    inner_rhs = jnp.moveaxis(right_side[:, :, 1:, :], 2, 0).reshape(inner_count, columns, radial)
    couple_first = jnp.zeros((inner_count, radial), jnp.float32).at[0].set(lower_diag[0])
    couple_last = (
        jnp.zeros((inner_count, radial), jnp.float32)
        .at[inner_count - 1]
        .set(upper_diag[inner_count - 1])
    )
    system = jnp.concatenate([inner_rhs, couple_first[:, None, :], couple_last[:, None, :]], axis=1)
    solution = cyclic_reduce(lower_diag, main_diag, upper_diag, system)
    inner_part = solution[:, :columns].reshape(inner_count, field_count, planes, radial)
    spread_first = solution[:, columns]
    spread_last = solution[:, columns + 1]
    sent_coefs = jnp.stack(
        [spread_first[inner_count - 1], spread_last[inner_count - 1], conduct[local_az - 1]]
    )
    prev_values, prev_coefs = shifted((inner_part[inner_count - 1], sent_coefs), "az", 1)
    low_sep = -prev_coefs[2]
    up_sep = -conduct[0]
    main_sep = 1.0 + prev_coefs[2] + conduct[0]
    coef_low = -low_sep * prev_coefs[0]
    coef_main = main_sep - low_sep * prev_coefs[1] - up_sep * spread_first[0]
    coef_high = -up_sep * spread_last[0]
    sep_coefs = jnp.stack([coef_low, coef_main, coef_high])
    sep_rhs = right_side[:, :, 0, :] - low_sep * prev_values - up_sep * inner_part[0]
    rounds = cycle_count.bit_length() - 1
    for doubling_step in range(rounds):
        stride = 1 << doubling_step
        behind = shifted((sep_coefs, sep_rhs), "az", stride)
        onward = shifted((sep_coefs, sep_rhs), "az", -stride)
        sep_coefs, sep_rhs = eliminate(sep_coefs, sep_rhs, behind, onward)
    separator = sep_rhs / jnp.sum(sep_coefs, axis=-2)[None, None, :]
    following = shifted(separator, "az", -1)
    interior = (
        inner_part
        - spread_first[:, None, None, :] * separator[None]
        - spread_last[:, None, None, :] * following[None]
    )
    assembled = jnp.concatenate([separator[None], interior], axis=0)
    return jnp.moveaxis(assembled, 0, 2)


def solution(mesh):
    return jax.shard_map(
        body,
        mesh=mesh,
        in_specs=(P(None, "ax", "az", None), P("az", None), P("ax", "az")),
        out_specs=P(None, "ax", "az", None),
        check_vma=False,
    )
```

profile of v0, /device:TPU:1, one launch (start us, length us, event | category | flops | bytes accessed | tf_op | source)
XLA Modules:
  0.0 435.8 jit_solution(16348824823411176151)
XLA Ops:
  6.5 2.1 slice.354
  16.4 30.4 %all_gather.10 = f32[128,64]{1,0:T(8,128)S(1)} all-gather(f32[16,64]{1,0:T(8,128)S(1)} %copy-done.29), channel_id=1, replica_groups=mesh['az'=16,'ax'=8] {'ax'}, dimensions={0}, use_global_device_ids=true | all-gather | bytes 36864 | tf_op jit(solution)/shard_map/all_gather | solution.py:92
  46.9 27.4 %all_gather.11 = f32[128,1024]{0,1:T(8,128)S(1)} all-gather(f32[128,64]{0,1:T(8,128)S(1)} %copy.29), channel_id=1, replica_groups=mesh['az'=16,'ax'=8] {'az'}, dimensions={1}, use_global_device_ids=true | all-gather | bytes 557056 | tf_op jit(solution)/shard_map/all_gather | solution.py:93
  74.5 2.8 copy.41
  78.3 1.8 multiply_add_fusion.5
  80.2 9.8 %all-gather.2.cloned.1.call-done = f32[3,8,1024,128]{3,2,1,0:T(8,128)} async-done(((f32[3,8,64,128]{3,2,1,0:T(8,128)}), f32[3,8,1024,128]{3,2,1,0:T(8,128)}) %all-gather.2.cloned.1.call-update) | async-done | bytes 12582928 | tf_op jit(solution)/shard_map/all_gather | solution.py:100
  90.1 12.7 %copy.28 = f32[3,8,1024,128]{2,1,0,3:T(8,128)} copy(f32[3,8,1024,128]{3,2,1,0:T(8,128)} %all-gather.2.cloned.1.call-done) | data formatting | bytes 25165824 | tf_op jit(solution)/shard_map/all_gather | solution.py:100
  102.8 249.0 %while.17 = (s32[]{:T(128)}, f32[4,3,8,64,32]{3,2,1,4,0:T(8,128)}, f32[4,3,8,1024,32]{3,2,1,4,0:T(8,128)}, f32[4,32,2048]{2,1,0:T(8,128)S(1)}, s32[]{:T(128)}, /*index=5*/s32[]{:T(128)}, s32[]{:T(128)}, s32[]{:T(128)}) while((s32[]{:T(128)}, f32[4,3,8,64,32]{3,2,1,4,0:T(8,128)}, f32[4,3,8,1024,32]{3,2,1,4,0:T(8,128)}, ...), condition=%wide.region_1.2_spmd, body=%wide.region_0.1_spmd.sunk | while | flops 603979776 | bytes 109256808 | solution.py:113
  103.7 4.6 %tile.15 = f32[32,65,1087]{2,1,0:T(8,128)} broadcast(f32[32,1087]{1,0:T(8,128)S(1)} %slice.661), dimensions={0,2} | broadcast | bytes 9182976 | tf_op jit(solution)/shard_map/while/body/eval_jaxpr/tile | solution.py:20
  108.3 8.8 %tile.16 = f32[32,70655]{1,0:T(8,128)} reshape(f32[32,65,1087]{2,1,0:T(8,128)} %tile.15) | data formatting | bytes 18087680 | tf_op jit(solution)/shard_map/while/body/eval_jaxpr/tile | solution.py:20
  117.1 7.6 %slice.662 = f32[32,69632]{1,0:T(8,128)} slice(f32[32,70655]{1,0:T(8,128)} %tile.16), slice={[0:32], [0:69632]} | slice | bytes 17825792 | tf_op jit(solution)/shard_map/while/body/eval_jaxpr/slice | solution.py:20
  124.7 9.7 %reshape.318 = f32[32,64,1088]{2,1,0:T(8,128)} reshape(f32[32,69632]{1,0:T(8,128)} %slice.662) | data formatting | bytes 17825792 | tf_op jit(solution)/shard_map/while/body/eval_jaxpr/reshape | solution.py:21
  134.4 8.4 %slice.663 = f32[32,64,1024]{2,1,0:T(8,128)} slice(f32[32,64,1088]{2,1,0:T(8,128)} %reshape.318), slice={[0:32], [0:64], [0:1024]} | slice | bytes 16777216 | tf_op jit(solution)/shard_map/while/body/eval_jaxpr/slice | solution.py:21
  142.8 11.9 %rev.17 = f32[32,64,1024]{2,1,0:T(8,128)} reverse(f32[32,64,1024]{2,1,0:T(8,128)} %slice.663), dimensions={1} | reverse | bytes 16777216 | tf_op jit(solution)/shard_map/while/body/eval_jaxpr/jit(_flip)/rev | solution.py:22
  154.7 10.3 %fusion.52 = f32[4,3,8,64,32]{3,2,1,4,0:T(8,128)} fusion(f32[4,3,8,64,32]{3,2,1,4,0:T(8,128)} %get-tuple-element.310, s32[]{:T(128)} %get-tuple-element.309, f32[32,64,1024]{2,1,0:T(8,128)} %rev.17, f32[4,3,8,1024,32]{3,2,1,4,0:T(8,128)} %get-tuple-element.319), kind=kOutput, calls=%fused_computation.5.clone.1 | convolution fusion | flops 603979776 | bytes 11928576 | tf_op jit(solution)/shard_map/while/body/eval_jaxpr/ijk,fxki->fxji/dot_general | solution.py:111
  165.9 4.6 %tile.15 = f32[32,65,1087]{2,1,0:T(8,128)} broadcast(f32[32,1087]{1,0:T(8,128)S(1)} %slice.661), dimensions={0,2} | broadcast | bytes 9182976 | tf_op jit(solution)/shard_map/while/body/eval_jaxpr/tile | solution.py:20
  170.5 8.8 %tile.16 = f32[32,70655]{1,0:T(8,128)} reshape(f32[32,65,1087]{2,1,0:T(8,128)} %tile.15) | data formatting | bytes 18087680 | tf_op jit(solution)/shard_map/while/body/eval_jaxpr/tile | solution.py:20
  179.3 7.6 %slice.662 = f32[32,69632]{1,0:T(8,128)} slice(f32[32,70655]{1,0:T(8,128)} %tile.16), slice={[0:32], [0:69632]} | slice | bytes 17825792 | tf_op jit(solution)/shard_map/while/body/eval_jaxpr/slice | solution.py:20
  186.9 9.7 %reshape.318 = f32[32,64,1088]{2,1,0:T(8,128)} reshape(f32[32,69632]{1,0:T(8,128)} %slice.662) | data formatting | bytes 17825792 | tf_op jit(solution)/shard_map/while/body/eval_jaxpr/reshape | solution.py:21
  196.6 8.4 %slice.663 = f32[32,64,1024]{2,1,0:T(8,128)} slice(f32[32,64,1088]{2,1,0:T(8,128)} %reshape.318), slice={[0:32], [0:64], [0:1024]} | slice | bytes 16777216 | tf_op jit(solution)/shard_map/while/body/eval_jaxpr/slice | solution.py:21
  205.0 11.9 %rev.17 = f32[32,64,1024]{2,1,0:T(8,128)} reverse(f32[32,64,1024]{2,1,0:T(8,128)} %slice.663), dimensions={1} | reverse | bytes 16777216 | tf_op jit(solution)/shard_map/while/body/eval_jaxpr/jit(_flip)/rev | solution.py:22
  216.9 10.4 %fusion.52 = f32[4,3,8,64,32]{3,2,1,4,0:T(8,128)} fusion(f32[4,3,8,64,32]{3,2,1,4,0:T(8,128)} %get-tuple-element.310, s32[]{:T(128)} %get-tuple-element.309, f32[32,64,1024]{2,1,0:T(8,128)} %rev.17, f32[4,3,8,1024,32]{3,2,1,4,0:T(8,128)} %get-tuple-element.319), kind=kOutput, calls=%fused_computation.5.clone.1 | convolution fusion | flops 603979776 | bytes 11928576 | tf_op jit(solution)/shard_map/while/body/eval_jaxpr/ijk,fxki->fxji/dot_general | solution.py:111
  228.2 4.6 %tile.15 = f32[32,65,1087]{2,1,0:T(8,128)} broadcast(f32[32,1087]{1,0:T(8,128)S(1)} %slice.661), dimensions={0,2} | broadcast | bytes 9182976 | tf_op jit(solution)/shard_map/while/body/eval_jaxpr/tile | solution.py:20
  232.8 8.8 %tile.16 = f32[32,70655]{1,0:T(8,128)} reshape(f32[32,65,1087]{2,1,0:T(8,128)} %tile.15) | data formatting | bytes 18087680 | tf_op jit(solution)/shard_map/while/body/eval_jaxpr/tile | solution.py:20
  241.6 7.6 %slice.662 = f32[32,69632]{1,0:T(8,128)} slice(f32[32,70655]{1,0:T(8,128)} %tile.16), slice={[0:32], [0:69632]} | slice | bytes 17825792 | tf_op jit(solution)/shard_map/while/body/eval_jaxpr/slice | solution.py:20
  249.2 9.7 %reshape.318 = f32[32,64,1088]{2,1,0:T(8,128)} reshape(f32[32,69632]{1,0:T(8,128)} %slice.662) | data formatting | bytes 17825792 | tf_op jit(solution)/shard_map/while/body/eval_jaxpr/reshape | solution.py:21
  258.9 8.4 %slice.663 = f32[32,64,1024]{2,1,0:T(8,128)} slice(f32[32,64,1088]{2,1,0:T(8,128)} %reshape.318), slice={[0:32], [0:64], [0:1024]} | slice | bytes 16777216 | tf_op jit(solution)/shard_map/while/body/eval_jaxpr/slice | solution.py:21
  267.3 11.9 %rev.17 = f32[32,64,1024]{2,1,0:T(8,128)} reverse(f32[32,64,1024]{2,1,0:T(8,128)} %slice.663), dimensions={1} | reverse | bytes 16777216 | tf_op jit(solution)/shard_map/while/body/eval_jaxpr/jit(_flip)/rev | solution.py:22
  279.2 10.3 %fusion.52 = f32[4,3,8,64,32]{3,2,1,4,0:T(8,128)} fusion(f32[4,3,8,64,32]{3,2,1,4,0:T(8,128)} %get-tuple-element.310, s32[]{:T(128)} %get-tuple-element.309, f32[32,64,1024]{2,1,0:T(8,128)} %rev.17, f32[4,3,8,1024,32]{3,2,1,4,0:T(8,128)} %get-tuple-element.319), kind=kOutput, calls=%fused_computation.5.clone.1 | convolution fusion | flops 603979776 | bytes 11928576 | tf_op jit(solution)/shard_map/while/body/eval_jaxpr/ijk,fxki->fxji/dot_general | solution.py:111
  290.4 4.6 %tile.15 = f32[32,65,1087]{2,1,0:T(8,128)} broadcast(f32[32,1087]{1,0:T(8,128)S(1)} %slice.661), dimensions={0,2} | broadcast | bytes 9182976 | tf_op jit(solution)/shard_map/while/body/eval_jaxpr/tile | solution.py:20
  295.0 8.8 %tile.16 = f32[32,70655]{1,0:T(8,128)} reshape(f32[32,65,1087]{2,1,0:T(8,128)} %tile.15) | data formatting | bytes 18087680 | tf_op jit(solution)/shard_map/while/body/eval_jaxpr/tile | solution.py:20
  303.8 7.6 %slice.662 = f32[32,69632]{1,0:T(8,128)} slice(f32[32,70655]{1,0:T(8,128)} %tile.16), slice={[0:32], [0:69632]} | slice | bytes 17825792 | tf_op jit(solution)/shard_map/while/body/eval_jaxpr/slice | solution.py:20
  311.4 9.7 %reshape.318 = f32[32,64,1088]{2,1,0:T(8,128)} reshape(f32[32,69632]{1,0:T(8,128)} %slice.662) | data formatting | bytes 17825792 | tf_op jit(solution)/shard_map/while/body/eval_jaxpr/reshape | solution.py:21
  321.1 8.4 %slice.663 = f32[32,64,1024]{2,1,0:T(8,128)} slice(f32[32,64,1088]{2,1,0:T(8,128)} %reshape.318), slice={[0:32], [0:64], [0:1024]} | slice | bytes 16777216 | tf_op jit(solution)/shard_map/while/body/eval_jaxpr/slice | solution.py:21
  329.5 11.9 %rev.17 = f32[32,64,1024]{2,1,0:T(8,128)} reverse(f32[32,64,1024]{2,1,0:T(8,128)} %slice.663), dimensions={1} | reverse | bytes 16777216 | tf_op jit(solution)/shard_map/while/body/eval_jaxpr/jit(_flip)/rev | solution.py:22
  341.4 10.4 %fusion.52 = f32[4,3,8,64,32]{3,2,1,4,0:T(8,128)} fusion(f32[4,3,8,64,32]{3,2,1,4,0:T(8,128)} %get-tuple-element.310, s32[]{:T(128)} %get-tuple-element.309, f32[32,64,1024]{2,1,0:T(8,128)} %rev.17, f32[4,3,8,1024,32]{3,2,1,4,0:T(8,128)} %get-tuple-element.319), kind=kOutput, calls=%fused_computation.5.clone.1 | convolution fusion | flops 603979776 | bytes 11928576 | tf_op jit(solution)/shard_map/while/body/eval_jaxpr/ijk,fxki->fxji/dot_general | solution.py:111
  351.8 2.0 copy.34
  354.4 1.8 copy.35
  359.8 1.5 multiply_add_fusion.3
  362.3 1.5 multiply_add_fusion.2
  364.9 1.2 multiply_add_fusion.1
  367.0 1.1 multiply_add_fusion
  369.2 1.1 add_divide_fusion
  370.5 1.1 collective-permute-done
  372.3 2.0 collective-permute-start.2
  374.4 2.4 collective-permute-start.4
  377.6 1.6 collective-permute-start.6
  379.2 6.3 %collective-permute-start.8 = (f32[3,512]{1,0:T(4,128)S(1)}, f32[3,512]{1,0:T(4,128)S(1)}, u32[]{:S(2)}, u32[]{:S(2)}) collective-permute-start(f32[3,512]{1,0:T(4,128)S(1)} %pad_maximum_fusion.4), channel_id=1, source_target_pairs={{16,0},{24,8},{32,16},{40,24},{48,32},{56,40},{64,48},{72,56},{80,... | collective-permute-start | bytes 18440 | tf_op jit(solution)/shard_map/ppermute | solution.py:14
  386.7 2.7 collective-permute-start.12
  390.4 1.7 collective-permute-start.14
  392.3 5.4 %collective-permute-start.1 = (f32[3,8,512]{2,1,0:T(8,128)S(1)}, f32[3,8,512]{2,1,0:T(8,128)S(1)}, u32[]{:S(2)}, u32[]{:S(2)}) collective-permute-start(f32[3,8,512]{2,1,0:T(8,128)S(1)} %bitcast.130), channel_id=1, source_target_pairs={{120,0},{0,8},{8,16},{16,24},{24,32},{32,40},{40,48},{48,56},{56,6... | collective-permute-start | bytes 147464 | tf_op jit(solution)/shard_map/ppermute | solution.py:14
  398.8 2.4 collective-permute-start.3
  401.3 1.2 collective-permute-done.3
  402.4 2.6 collective-permute-done.5
  405.1 1.9 collective-permute-start.7
  407.0 2.5 collective-permute-start.9
  409.5 1.4 collective-permute-done.7
  411.0 2.7 collective-permute-start.13
  413.7 1.5 collective-permute-done.11
  415.2 1.8 collective-permute-start.15
  417.0 2.7 collective-permute-done.15
  419.7 3.7 collective-permute-start.16
  424.0 2.3 collective-permute-done.16
  426.9 2.1 maximum_bitcast_fusion
  (172 shorter events, 26.7 us)
Async XLA Ops:
  6.5 2.2 copy-start.22
  6.5 83.5 %all-gather.2.cloned.1.call-start = ((), (), s32[]{:S(2)}) async-start(), calls=%async_computation | async-start | bytes 13369344 | tf_op jit(solution)/shard_map/all_gather | solution.py:100
  10.2 0.8 copy-start.13
  11.0 0.6 copy-start.1
  11.1 0.7 copy-start.3
  11.3 3.9 copy-start.5
  11.3 3.8 copy-start.7
  11.3 5.1 %copy-start.29 = (f32[16,64]{1,0:T(8,128)S(1)}, f32[16,64]{1,0:T(8,128)}, u32[]{:S(2)}) copy-start(f32[16,64]{1,0:T(8,128)} %param.15) | copy-start | bytes 12292
  11.5 63.0 %slice-start = ((f32[3,8,64,512]{3,2,1,0:T(8,128)}), f32[3,8,64,384]{3,2,1,0:T(8,128)S(1)}, s32[]{:S(2)}) async-start(f32[3,8,64,512]{3,2,1,0:T(8,128)} %param.13), calls=%async_computation.1 | async-start | bytes 4718592 | tf_op jit(solution)/shard_map/slice | solution.py:115
  11.7 35.2 %copy-start.9 = (f32[64,512]{1,0:T(8,128)}, f32[64,512]{1,0:T(8,128)S(1)}, u32[]{:S(2)}) copy-start(f32[64,512]{1,0:T(8,128)S(1)} %get-tuple-element.193) | copy-start | bytes 393220
  11.7 3.4 copy-start.11
  13.2 2.0 copy-start.19
  15.2 0.6 copy-start.21
  74.5 2.8 copy-start.15
  74.5 2.8 copy-start.17
  74.5 3.8 copy-start.20
  351.8 2.1 copy-start
  354.4 1.8 copy-start.27
  354.4 1.8 copy-start.28
  356.8 0.9 copy-start.14
  356.8 1.0 copy-start.23
  358.8 1.0 copy-start.2
  358.9 1.0 copy-start.4
  361.4 1.0 copy-start.6
  361.4 1.0 copy-start.8
  363.9 0.9 copy-start.10
  363.9 1.0 copy-start.12
  366.1 0.9 copy-start.16
  366.1 1.0 copy-start.18
  368.2 0.9 copy-start.24
  368.2 1.0 copy-start.25
  368.2 1.0 copy-start.26
  369.2 1.1 copy-start.30
  370.4 1.2 collective-permute-start
  372.3 5.0 %collective-permute-start.2 = (f32[3,512]{1,0:T(4,128)S(1)}, f32[3,512]{1,0:T(4,128)S(1)}, u32[]{:S(2)}, u32[]{:S(2)}) collective-permute-start(f32[3,512]{1,0:T(4,128)S(1)} %pad_maximum_fusion.3), channel_id=1, source_target_pairs={{120,0},{0,8},{8,16},{16,24},{24,32},{32,40},{40,48},{48,56},{56,6... | collective-permute-start | bytes 18440 | tf_op jit(solution)/shard_map/ppermute | solution.py:14
  374.4 3.2 collective-permute-start.4
  377.6 8.8 %collective-permute-start.6 = (f32[3,512]{1,0:T(4,128)S(1)}, f32[3,512]{1,0:T(4,128)S(1)}, u32[]{:S(2)}, u32[]{:S(2)}) collective-permute-start(f32[3,512]{1,0:T(4,128)S(1)} %pad_maximum_fusion.4), channel_id=1, source_target_pairs={{112,0},{120,8},{0,16},{8,24},{16,32},{24,40},{32,48},{40,56},{48,... | collective-permute-start | bytes 18440 | tf_op jit(solution)/shard_map/ppermute | solution.py:14
  379.2 7.3 %collective-permute-start.8 = (f32[3,512]{1,0:T(4,128)S(1)}, f32[3,512]{1,0:T(4,128)S(1)}, u32[]{:S(2)}, u32[]{:S(2)}) collective-permute-start(f32[3,512]{1,0:T(4,128)S(1)} %pad_maximum_fusion.4), channel_id=1, source_target_pairs={{16,0},{24,8},{32,16},{40,24},{48,32},{56,40},{64,48},{72,56},{80,... | collective-permute-start | bytes 18440 | tf_op jit(solution)/shard_map/ppermute | solution.py:14
  386.6 3.8 collective-permute-start.10
  386.7 3.7 collective-permute-start.12
  390.4 7.2 %collective-permute-start.14 = (f32[3,512]{1,0:T(4,128)S(1)}, f32[3,512]{1,0:T(4,128)S(1)}, u32[]{:S(2)}, u32[]{:S(2)}) collective-permute-start(f32[3,512]{1,0:T(4,128)S(1)} %pad_maximum_fusion.6), channel_id=1, source_target_pairs={{64,0},{72,8},{80,16},{88,24},{96,32},{104,40},{112,48},{120,56},{... | collective-permute-start | bytes 18440 | tf_op jit(solution)/shard_map/ppermute | solution.py:14
  392.3 6.5 %collective-permute-start.1 = (f32[3,8,512]{2,1,0:T(8,128)S(1)}, f32[3,8,512]{2,1,0:T(8,128)S(1)}, u32[]{:S(2)}, u32[]{:S(2)}) collective-permute-start(f32[3,8,512]{2,1,0:T(8,128)S(1)} %bitcast.130), channel_id=1, source_target_pairs={{120,0},{0,8},{8,16},{16,24},{24,32},{32,40},{40,48},{48,56},{56,6... | collective-permute-start | bytes 147464 | tf_op jit(solution)/shard_map/ppermute | solution.py:14
  398.8 3.6 collective-permute-start.3
  401.2 3.8 collective-permute-start.5
  405.1 5.9 %collective-permute-start.7 = (f32[3,8,512]{2,1,0:T(8,128)S(1)}, f32[3,8,512]{2,1,0:T(8,128)S(1)}, u32[]{:S(2)}, u32[]{:S(2)}) collective-permute-start(f32[3,8,512]{2,1,0:T(8,128)S(1)} %multiply_subtract_fusion.3), channel_id=1, source_target_pairs={{112,0},{120,8},{0,16},{8,24},{16,32},{24,40},{32,48},{40,56},{48,... | collective-permute-start | bytes 147464 | tf_op jit(solution)/shard_map/ppermute | solution.py:14
  407.0 3.9 collective-permute-start.9
  410.9 4.2 collective-permute-start.11
  411.0 4.1 collective-permute-start.13
  415.2 4.5 %collective-permute-start.15 = (f32[3,8,512]{2,1,0:T(8,128)S(1)}, f32[3,8,512]{2,1,0:T(8,128)S(1)}, u32[]{:S(2)}, u32[]{:S(2)}) collective-permute-start(f32[3,8,512]{2,1,0:T(8,128)S(1)} %multiply_subtract_fusion.1), channel_id=1, source_target_pairs={{64,0},{72,8},{80,16},{88,24},{96,32},{104,40},{112,48},{120,56},{... | collective-permute-start | bytes 147464 | tf_op jit(solution)/shard_map/ppermute | solution.py:14
  419.7 6.5 %collective-permute-start.16 = (f32[3,8,512]{2,1,0:T(8,128)S(1)}, f32[3,8,512]{2,1,0:T(8,128)S(1)}, u32[]{:S(2)}, u32[]{:S(2)}) collective-permute-start(f32[3,8,512]{2,1,0:T(8,128)S(1)} %subtract_divide_fusion), channel_id=1, source_target_pairs={{8,0},{16,8},{24,16},{32,24},{40,32},{48,40},{56,48},{64,56},{72,6... | collective-permute-start | bytes 147464 | tf_op jit(solution)/shard_map/ppermute | solution.py:14
Sparse Core Ops, SparseCore 0:
  9.0 80.9 all-gather.1
where the time goes:
time: 438 us; the launch traced here: 436 us
  local copies, waits for them, and re-layouts  241 us (55%)
  blocking collectives  57.8 us (13%)
  matrix products  41.4 us (9%)
  starting transfers between devices  37.3 us (9%)
  waiting for transfers between devices  25.9 us (6%)
  other arithmetic  18.4 us (4%)
  between operations  14.3 us (3%)
    another operation x8, local copies, waits for them, and re-layouts, toeplitz_rows(): tiled = jnp.tile(flipped, (1, rows + 1))[:, :rows * (length + 1)]  53.5 us
    rev x4, local copies, waits for them, and re-layouts, toeplitz_rows(): return jnp.flip(sliding, axis=1)  47.6 us
    dot_general x4, matrix products, one_group(): jnp.einsum('ijk,fxki->fxji', circulant, piece_part, precision=lax.Precisi...  41.4 us
    reshape x4, local copies, waits for them, and re-layouts, toeplitz_rows(): sliding = tiled.reshape(window.shape[0], rows, length + 1)[:, :, :cols]  38.8 us
    ppermute x17, starting transfers between devices, shifted(): return lax.ppermute(block, axis, route)  37.3 us
    slice x4, local copies, waits for them, and re-layouts, toeplitz_rows(): sliding = tiled.reshape(window.shape[0], rows, length + 1)[:, :, :cols]  33.6 us
    slice x4, local copies, waits for them, and re-layouts, toeplitz_rows(): tiled = jnp.tile(flipped, (1, rows + 1))[:, :rows * (length + 1)]  30.5 us
    all_gather x1, blocking collectives, body(): gathered_cycles = lax.all_gather(kernel, 'ax', axis=0, tiled=True)  30.4 us
  transfers between devices with their start and end apart: 18, of which 13 were waited for; matrix products, arithmetic and copies ran while one was open for 3% of the time, Pallas kernels for 0%

commit v1 on v0

v1 whole, which is shorter than its diff:
```python
import functools

import jax
import jax.numpy as jnp
import ml_dtypes
import numpy as np
from jax import lax
from jax.experimental import pallas as pl
from jax.experimental.pallas import tpu as pltpu
from jax.sharding import PartitionSpec as P

MESH = pl.DeviceIdType.MESH
F32 = jnp.float32
BF16 = jnp.bfloat16

NF = 3
NX = 8
NB = 64
NQ = 16
HALF = NB * NQ // 2
NEAR = 128
FAR_TILES = 3
FAR = NF * FAR_TILES
OFFSETS = (0, 32, 48, 56, 60, 62)
ORDER = (8, 4, 12, 1, 9, 5, 13, 2, 10, 6, 14, 3, 11, 7, 15)


def split_const(matrix):
    high = matrix.astype(ml_dtypes.bfloat16)
    low = (matrix - high.astype(np.float64)).astype(ml_dtypes.bfloat16)
    return high, low


def transforms():
    points = 2 * HALF
    j = np.arange(HALF)
    forward, inverse = [], []
    for odd in (0, 1):
        freq = 2 * np.arange(HALF // 2) + odd
        angle = 2.0 * np.pi * ((freq[:, None] * j[None, :]) % points) / points
        real, imag = np.cos(angle), -np.sin(angle)
        scale = np.full((HALF // 2, 1), 2.0 / points)
        real_back, imag_back = real * scale, imag * scale
        if not odd:
            imag[0] = np.cos(np.pi * j)
            real_back[0] = 1.0 / points
            imag_back[0] = imag[0] / points
        forward.append(np.concatenate([real, imag]))
        inverse.append(np.concatenate([real_back, imag_back]))
    order = (NB * np.arange(8)[None, :] + np.arange(NB)[:, None]).reshape(-1)
    back = np.concatenate(inverse, axis=0).T[order]
    even_high, even_low = split_const(forward[0])
    odd_high, odd_low = split_const(forward[1])
    back_high, back_low = split_const(back)
    return np.stack([even_high, even_low, odd_high, odd_low]), np.stack([back_high, back_low])


def split(x):
    high = x.astype(BF16)
    return high, (x - high.astype(F32)).astype(BF16)


def forward_transform(dft_ref, which, rows):
    high, low = split(rows)
    both = jnp.concatenate([high, low], axis=0)
    contract = (((1,), (1,)), ((), ()))
    one = lax.dot_general(dft_ref[2 * which], both, contract, preferred_element_type=F32)
    two = lax.dot_general(dft_ref[2 * which + 1], high, contract, preferred_element_type=F32)
    return one[:, :128] + one[:, 128:] + two


def inverse_transform(idft_ref, spectrum):
    high, low = split(spectrum)
    both = jnp.concatenate([high, low], axis=1)
    contract = (((1,), (0,)), ((), ()))
    one = lax.dot_general(idft_ref[0], both, contract, preferred_element_type=F32)
    two = lax.dot_general(idft_ref[1], high, contract, preferred_element_type=F32)
    return one[:, :128] + one[:, 128:] + two


def coefficients(links, store):
    excess = jnp.ones(links.shape, F32)
    onward = None
    for level in range(6):
        count = links.shape[0] // 2
        pairs = links.reshape(count, 2, 8, 128)
        behind, ahead = pairs[:, 0], pairs[:, 1]
        own = excess.reshape(count, 2, 8, 128)
        inv = 1.0 / (behind + ahead + own[:, 1])
        alpha, beta = behind * inv, ahead * inv
        store(OFFSETS[level], alpha, beta, inv)
        to_left, to_right = alpha * own[:, 1], beta * own[:, 1]
        excess = own[:, 0] + to_left
        if count > 1:
            excess = jnp.concatenate([excess[:1], excess[1:] + to_right[:-1]], axis=0)
        onward = to_right[count - 1] if onward is None else onward + to_right[count - 1]
        links = behind * beta
    return links[0], excess[0], onward


def reduce_block(values, load, keep):
    onward = None
    for level in range(6):
        count = values.shape[0] // 2
        pairs = values.reshape(count, 2, 8, 128)
        even, odd = pairs[:, 0], pairs[:, 1]
        keep(OFFSETS[level], odd)
        alpha, beta, _ = load(OFFSETS[level], count)
        to_right = beta * odd
        values = even + alpha * odd
        if count > 1:
            values = jnp.concatenate([values[:1], values[1:] + to_right[:-1]], axis=0)
        onward = to_right[count - 1] if onward is None else onward + to_right[count - 1]
    return values[0], onward


def expand_block(first, following, load, kept):
    solved = first[None]
    for level in reversed(range(6)):
        count = 32 >> level
        alpha, beta, inv = load(OFFSETS[level], count)
        right = following[None]
        if count > 1:
            right = jnp.concatenate([solved[1:], right], axis=0)
        odd = inv * kept(OFFSETS[level], count) + alpha * solved + beta * right
        solved = jnp.stack([solved, odd], axis=1).reshape(2 * count, 8, 128)
    return solved


def ring_coefficients(link, first, onward, prev, ahead):
    excess = first + prev(onward, 1)
    after, before = link, prev(link, 1)
    levels = []
    for d in (1, 2, 4, 8):
        inv = 1.0 / (excess + before + after)
        alpha, beta = before * prev(inv, d), after * ahead(inv, d)
        levels.append((alpha, beta))
        excess = excess + alpha * prev(excess, d) + beta * ahead(excess, d)
        if d < 8:
            before, after = alpha * prev(before, d), beta * ahead(after, d)
    return levels, 1.0 / excess


def ring_solve(first, onward, levels, final, prev, ahead):
    value = first + prev(onward, 1)
    for d, (alpha, beta) in zip((1, 2, 4, 8), levels):
        value = value + alpha * prev(value, d) + beta * ahead(value, d)
    return value * final


def far_prev(v, d):
    return jnp.concatenate([v[NQ - d :], v[: NQ - d]], axis=0)


def far_ahead(v, d):
    return jnp.concatenate([v[d:], v[:d]], axis=0)


def near_prev(v, d):
    if d == 8:
        return pltpu.roll(v, 64, 1)
    rolled = pltpu.roll(v, d, 0)
    row = lax.broadcasted_iota(jnp.int32, (8, 128), 0)
    return jnp.where(row >= d, rolled, pltpu.roll(rolled, 64, 1))


def near_ahead(v, d):
    if d == 8:
        return pltpu.roll(v, 64, 1)
    rolled = pltpu.roll(v, 8 - d, 0)
    row = lax.broadcasted_iota(jnp.int32, (8, 128), 0)
    return jnp.where(row < 8 - d, rolled, pltpu.roll(rolled, 64, 1))


def swap_halves(x):
    return pltpu.roll(x, 64, x.ndim - 1)


def kernel_body(
    fields, conduct, kernel, dft, idft, out,
    held, done, dft_v, idft_v, near_send, near_recv, back_send, back_recv,
    kernel_pad, kernel_recv, conduct_send, conduct_recv, link_rows, spectrum,
    alpha_ref, beta_ref, inv_ref, ring_ref, odd_ref, work,
    far_send, far_recv, sep_send, sep_recv,
    load_sem, const_sem, store_sem, ns, nr, bs, br, ks, kr, cs, cr, fs, fr, ss, sr,
):
    me = lax.axis_index("az")
    mx = lax.axis_index("ax")
    blocks = kernel.shape[0] // 8
    ax_count = lax.axis_size("ax")
    my_group = me // blocks

    def peer(k):
        return lax.rem(me + k, NQ)

    def source(k):
        return lax.rem(me + NQ - k, NQ)

    loads = {}
    for tile in range(4):
        for f in range(NF):
            copy = pltpu.make_async_copy(
                fields.at[f, :, pl.ds(128 * tile, 128)], held.at[f * 4 + tile], load_sem.at[f * 4 + tile]
            )
            loads[f, tile] = copy
            if tile == 0:
                copy.start()
    const_loads = [
        pltpu.make_async_copy(dft, dft_v, const_sem.at[0]),
        pltpu.make_async_copy(idft, idft_v, const_sem.at[1]),
    ]

    barrier = pltpu.get_barrier_semaphore()
    for k in ORDER:
        pl.semaphore_signal(barrier, inc=1, device_id={"az": peer(k), "ax": mx}, device_id_type=MESH)
    for k in range(1, NQ):
        pl.semaphore_signal(barrier, inc=1, device_id={"az": peer(k), "ax": my_group}, device_id_type=MESH)

    @pl.when(my_group != mx)
    def _():
        pl.semaphore_signal(barrier, inc=1, device_id={"az": me, "ax": my_group}, device_id_type=MESH)

    for copy in const_loads:
        copy.start()
    for tile in range(1, 4):
        for f in range(NF):
            loads[f, tile].start()

    kernel_pad[...] = jnp.concatenate([kernel[...], jnp.zeros(kernel.shape, F32)], axis=1).reshape(blocks, 8, 128)
    near_links = conduct[:, :NEAR]
    conduct_send[...] = jnp.concatenate([near_links, near_links], axis=0).T.reshape(NQ, 8, 128)
    conduct_recv[me] = conduct_send[me]

    def transpose_near(f):
        loads[f, 0].wait()
        for k in range(4):
            near_send[f, :, k] = held[f * 4, 128 * k : 128 * k + 128, :].T.reshape(NQ, 8, 128)
        near_recv[f, me] = near_send[f, me]

    transpose_near(0)

    incoming = 15 + blocks * ax_count - jnp.where(my_group == mx, 1, 0)
    pl.semaphore_wait(barrier, incoming)

    def kernel_copy(b, dq):
        return pltpu.make_async_remote_copy(
            kernel_pad.at[b], kernel_recv.at[me], ks.at[b, dq], kr.at[me],
            device_id={"az": blocks * mx + b, "ax": lax.rem(mx + dq, ax_count)}, device_id_type=MESH,
        )

    for b in range(blocks):
        for dq in range(ax_count):
            if dq:
                kernel_copy(b, dq).start()
            else:

                @pl.when(me == blocks * mx + b)
                def _():
                    kernel_recv[me] = kernel_pad[b]

                @pl.when(me != blocks * mx + b)
                def _():
                    kernel_copy(b, 0).start()

    def near_copy(f, k, slot):
        return pltpu.make_async_remote_copy(
            near_send.at[f, peer(k)], near_recv.at[f, slot], ns.at[f, k], nr.at[f, k],
            device_id={"az": peer(k), "ax": mx}, device_id_type=MESH,
        )

    def conduct_copy(k, slot):
        return pltpu.make_async_remote_copy(
            conduct_send.at[peer(k)], conduct_recv.at[slot], cs.at[k], cr.at[k],
            device_id={"az": peer(k), "ax": mx}, device_id_type=MESH,
        )

    for k in ORDER:
        near_copy(0, k, me).start()
    for k in ORDER:
        conduct_copy(k, me).start()
    for f in (1, 2):
        transpose_near(f)
        for k in ORDER:
            near_copy(f, k, me).start()

    def coefficient_store(c):
        def store(offset, alpha, beta, inv):
            count = alpha.shape[0]
            alpha_ref[c, offset : offset + count] = alpha
            beta_ref[c, offset : offset + count] = beta
            inv_ref[c, offset : offset + count] = inv

        return store

    def coefficient_load(c):
        def load(offset, count):
            return (
                alpha_ref[c, offset : offset + count],
                beta_ref[c, offset : offset + count],
                inv_ref[c, offset : offset + count],
            )

        return load

    def odd_keep(w):
        def keep(offset, value):
            odd_ref[w, offset : offset + value.shape[0]] = value

        return keep

    def odd_load(w):
        return lambda offset, count: odd_ref[w, offset : offset + count]

    row = lax.broadcasted_iota(jnp.int32, (8, 128), 0)

    def far_coefficients(lt, carry):
        lanes = pl.ds(pl.multiple_of(128 * lt + NEAR, 128), 128)
        links = jnp.stack([jnp.broadcast_to(conduct[j : j + 1, lanes], (8, 128)) for j in range(NB)])
        link, first, onward = coefficients(links, coefficient_store(lt + 1))
        tile = jnp.where(row == 0, link, jnp.where(row == 1, first, onward))
        for f in range(NF):
            far_send[f * FAR_TILES + lt, 2] = tile
        return carry

    lax.fori_loop(0, FAR_TILES, far_coefficients, 0)

    for f in range(NF):
        for tile in range(1, 4):
            loads[f, tile].wait()

    def far_index(w):
        return w // FAR_TILES, lax.rem(w, FAR_TILES)

    def far_reduce(w, carry):
        f, lt = far_index(w)
        values = jnp.stack([held[f * 4 + lt + 1, pl.ds(j, 8, stride=NB), :] for j in range(NB)])
        first, onward = reduce_block(values, coefficient_load(lt + 1), odd_keep(w))
        far_send[w, 0] = first
        far_send[w, 1] = onward
        return carry

    lax.fori_loop(0, FAR, far_reduce, 0)

    def owner(w):
        return 2 * w if w < 8 else 1

    def far_copy(w):
        return pltpu.make_async_remote_copy(
            far_send.at[w], far_recv.at[me], fs.at[w], fr.at[me],
            device_id={"az": owner(w), "ax": mx}, device_id_type=MESH,
        )

    for w in range(FAR):

        @pl.when(me == owner(w))
        def _():
            far_recv[me] = far_send[w]

        @pl.when(me != owner(w))
        def _():
            far_copy(w).start()

    for k in range(NQ):

        def wait_kernel():
            pltpu.make_async_remote_copy(
                kernel_pad.at[0], kernel_recv.at[source(k)], ks.at[0, 0], kr.at[source(k)],
                device_id={"az": source(k), "ax": my_group}, device_id_type=MESH,
            ).wait_recv()

        if k:
            wait_kernel()
        else:
            pl.when(my_group != mx)(wait_kernel)
    for copy in const_loads:
        copy.wait()

    lane = lax.broadcasted_iota(jnp.int32, (8, 128), 1)
    pieces = kernel_recv[...].reshape(8, 2, 8, 128)
    lags = jnp.where(lane[None] < 64, pieces[:, 0], swap_halves(pieces[:, 1].reshape(64, 128)).reshape(8, 8, 128))
    total, difference = lags[:4] + lags[4:], lags[:4] - lags[4:]
    for odd, part in enumerate((total, difference)):
        rows = jnp.concatenate([part[m] for m in range(4)], axis=1)
        rows = jnp.concatenate([rows] * 16, axis=0)
        transformed = forward_transform(dft_v, odd, rows)
        real, imag = transformed[:256], transformed[256:]
        if odd:
            spectrum[3] = real
            spectrum[4] = imag
        else:
            first_row = lax.broadcasted_iota(jnp.int32, (256, 128), 0) == 0
            spectrum[0] = real
            spectrum[1] = jnp.where(first_row, 0.0, imag)
            spectrum[2] = jnp.where(first_row, imag, real)

    for k in ORDER:
        conduct_copy(k, source(k)).wait_recv()
    for s in range(8):
        rows = jnp.concatenate([conduct_recv[s]] * 8 + [conduct_recv[8 + s]] * 8, axis=0)
        link_rows[pl.ds(s, NB, stride=8), :] = rows.T[:NB]
    link, first, onward = coefficients(link_rows[...].reshape(NB, 8, 128), coefficient_store(0))
    levels, final = ring_coefficients(link, first, onward, near_prev, near_ahead)
    for index, (alpha, beta) in enumerate(levels):
        ring_ref[2 * index] = alpha
        ring_ref[2 * index + 1] = beta
    ring_ref[8] = final

    def back_copy(f, k, slot):
        return pltpu.make_async_remote_copy(
            back_send.at[f, peer(k)], back_recv.at[f, :, slot], bs.at[f, k], br.at[f, k],
            device_id={"az": peer(k), "ax": mx}, device_id_type=MESH,
        )

    def near_solve(f):
        for k in ORDER:
            near_copy(f, k, source(k)).wait_recv()
        pieces = near_recv[f].reshape(8, 2, 4, 8, 128)
        low, high = pieces[:, 0].reshape(256, 128), pieces[:, 1].reshape(256, 128)
        left = lax.broadcasted_iota(jnp.int32, (256, 128), 1) < 64
        plane_a = jnp.where(left, low, swap_halves(high)).reshape(8, 4, 8, 128)
        plane_b = jnp.where(left, swap_halves(low), high).reshape(8, 4, 8, 128)
        points = jnp.stack([plane_a, plane_b], axis=2).reshape(8, 64, 128)
        total, difference = points[:4] + points[4:], points[:4] - points[4:]
        total = jnp.concatenate([total[m] for m in range(4)], axis=1)
        difference = jnp.concatenate([difference[m] for m in range(4)], axis=1)
        even = forward_transform(dft_v, 0, jnp.concatenate([total, total], axis=0))
        odd = forward_transform(dft_v, 1, jnp.concatenate([difference, -difference], axis=0))
        real, imag = even[:256], even[256:]
        odd_real, odd_imag = odd[:256], odd[256:]
        product = jnp.concatenate(
            [
                real * spectrum[0] - imag * spectrum[1],
                real * spectrum[1] + imag * spectrum[2],
                odd_real * spectrum[3] - odd_imag * spectrum[4],
                odd_real * spectrum[4] + odd_imag * spectrum[3],
            ],
            axis=0,
        )
        filtered = inverse_transform(idft_v, product).reshape(NB, 8, 128)
        first, onward = reduce_block(filtered, coefficient_load(0), odd_keep(FAR))
        ring = [(ring_ref[2 * i], ring_ref[2 * i + 1]) for i in range(4)]
        first = ring_solve(first, onward, ring, ring_ref[8], near_prev, near_ahead)
        solved = expand_block(first, near_ahead(first, 1), coefficient_load(0), odd_load(FAR))
        work[...] = solved.reshape(512, 128)
        for s in range(8):
            part = work[pl.ds(s, NB, stride=8), :]
            tiles = jnp.concatenate([part, pltpu.roll(part, 120, 1)], axis=0).T
            tiles = tiles.reshape(2, 4, 2, 8, 128)[:, :, 0]
            back_send[f, s] = tiles[0]
            back_send[f, 8 + s] = tiles[1]
        back_recv[f, :, me] = back_send[f, me]
        for k in ORDER:
            back_copy(f, k, me).start()

    sep_owner = jnp.logical_or(lax.rem(me, 2) == 0, me == 1)
    my_item = jnp.where(me == 1, 8, me // 2)

    def sep_copy(k, w):
        return pltpu.make_async_remote_copy(
            sep_send.at[peer(k)], sep_recv.at[w], ss.at[k], sr.at[w],
            device_id={"az": peer(k), "ax": mx}, device_id_type=MESH,
        )

    def far_ring():
        for k in range(1, NQ):
            pltpu.make_async_remote_copy(
                far_send.at[0], far_recv.at[source(k)], fs.at[0], fr.at[source(k)],
                device_id={"az": source(k), "ax": mx}, device_id_type=MESH,
            ).wait_recv()
        spread = [jnp.broadcast_to(far_recv[:, 2, i : i + 1, :], (NQ, 8, 128)) for i in range(3)]
        levels, final = ring_coefficients(*spread, far_prev, far_ahead)
        value = ring_solve(far_recv[:, 0], far_recv[:, 1], levels, final, far_prev, far_ahead)
        sep_send[:, 0] = value
        sep_send[:, 1] = far_ahead(value, 1)
        sep_recv[my_item] = sep_send[me]
        for k in ORDER:
            sep_copy(k, my_item).start()

    stores = {}
    for f in range(NF):
        for tile in range(4):
            stores[f, tile] = pltpu.make_async_copy(
                done.at[f * 4 + tile], out.at[f, :, pl.ds(128 * tile, 128)], store_sem.at[f * 4 + tile]
            )

    near_solve(0)
    pl.when(sep_owner)(far_ring)
    near_solve(1)

    for w in range(FAR):

        @pl.when(me != owner(w))
        def _():
            pltpu.make_async_remote_copy(
                sep_send.at[0], sep_recv.at[w], ss.at[0], sr.at[w],
                device_id={"az": owner(w), "ax": mx}, device_id_type=MESH,
            ).wait_recv()

    def far_expand(w, carry):
        f, lt = far_index(w)
        solved = expand_block(sep_recv[w, 0], sep_recv[w, 1], coefficient_load(lt + 1), odd_load(w))
        for j in range(NB):
            done[f * 4 + lt + 1, pl.ds(j, 8, stride=NB), :] = solved[j]
        return carry

    lax.fori_loop(0, FAR, far_expand, 0)
    for f in range(NF):
        for tile in range(1, 4):
            stores[f, tile].start()

    near_solve(2)

    for f in range(NF):
        for k in ORDER:
            back_copy(f, k, source(k)).wait_recv()
        for k in range(4):
            done[f * 4, 128 * k : 128 * k + 128, :] = back_recv[f, k].reshape(128, 128).T
        stores[f, 0].start()

    for b in range(blocks):
        for dq in range(ax_count):
            if dq:
                kernel_copy(b, dq).wait_send()
            else:

                @pl.when(me != blocks * mx + b)
                def _():
                    kernel_copy(b, 0).wait_send()

    for k in ORDER:
        conduct_copy(k, me).wait_send()
        for f in range(NF):
            near_copy(f, k, me).wait_send()
            back_copy(f, k, me).wait_send()
    for w in range(FAR):

        @pl.when(me != owner(w))
        def _():
            far_copy(w).wait_send()

    @pl.when(sep_owner)
    def _():
        for k in ORDER:
            sep_copy(k, my_item).wait_send()

    for copy in stores.values():
        copy.wait()


def body(fields, conduct, kernel):
    dft, idft = transforms()
    shape = fields.shape
    flat = fields.reshape(NF, NX * NB, shape[3])
    blocks = kernel.shape[0] // 8
    vmem = pltpu.VMEM
    dma = pltpu.SemaphoreType.DMA
    anywhere = pl.BlockSpec(memory_space=pl.ANY)
    inside = pl.BlockSpec(memory_space=pltpu.VMEM)
    out = pl.pallas_call(
        kernel_body,
        out_shape=jax.ShapeDtypeStruct(flat.shape, F32),
        in_specs=[anywhere, inside, inside, anywhere, anywhere],
        out_specs=anywhere,
        scratch_shapes=[
            vmem((12, 512, 128), F32),
            vmem((12, 512, 128), F32),
            vmem((4, 512, 512), BF16),
            vmem((2, 512, 1024), BF16),
            vmem((NF, NQ, 4, 8, 128), F32),
            vmem((NF, NQ, 4, 8, 128), F32),
            vmem((NF, NQ, 4, 8, 128), F32),
            vmem((NF, 4, NQ, 8, 128), F32),
            vmem((blocks, 8, 128), F32),
            vmem((NQ, 8, 128), F32),
            vmem((NQ, 8, 128), F32),
            vmem((NQ, 8, 128), F32),
            vmem((512, 128), F32),
            vmem((5, 256, 128), F32),
            vmem((4, 64, 8, 128), F32),
            vmem((4, 64, 8, 128), F32),
            vmem((4, 64, 8, 128), F32),
            vmem((9, 8, 128), F32),
            vmem((FAR + 1, 64, 8, 128), F32),
            vmem((512, 128), F32),
            vmem((FAR, 3, 8, 128), F32),
            vmem((NQ, 3, 8, 128), F32),
            vmem((NQ, 2, 8, 128), F32),
            vmem((FAR, 2, 8, 128), F32),
            dma((12,)), dma((2,)), dma((12,)),
            dma((NF, NQ)), dma((NF, NQ)), dma((NF, NQ)), dma((NF, NQ)),
            dma((blocks, lax.axis_size("ax"))), dma((NQ,)),
            dma((NQ,)), dma((NQ,)),
            dma((FAR,)), dma((NQ,)),
            dma((NQ,)), dma((FAR,)),
        ],
        compiler_params=pltpu.CompilerParams(
            collective_id=0, has_side_effects=True, vmem_limit_bytes=50 * 2**20
        ),
    )(flat, conduct, kernel, jnp.asarray(dft), jnp.asarray(idft))
    return out.reshape(shape)


def solution(mesh):
    return jax.shard_map(
        body,
        mesh=mesh,
        in_specs=(P(None, "ax", "az", None), P("az", None), P("ax", "az")),
        out_specs=P(None, "ax", "az", None),
        check_vma=False,
    )
```

time: 438 us -> 52 us (0.12)
  local copies, waits for them, and re-layouts: 241 us -> 7.22 us
  blocking collectives: 57.8 us -> 0 us
  Pallas kernels: 0 us -> 44.5 us
  matrix products: 41.4 us -> 0 us
  starting transfers between devices: 37.3 us -> 0 us
  waiting for transfers between devices: 25.9 us -> 0 us
  other arithmetic: 18.4 us -> 0 us
  between operations: 14.3 us -> 0.01 us
    slice x38 -> x0, local copies, waits for them, and re-layouts: 74.9 us -> none  [the longest x4 33.6 us: toeplitz_rows(): sliding = tiled.reshape(window.shape[0], rows, length + 1)[:, :, :cols]]
    all_gather x2 -> x0, blocking collectives: 57.8 us -> none  [the longest x1 30.4 us: body(): gathered_cycles = lax.all_gather(kernel, 'ax', axis=0, tiled=True)]
    another operation x9 -> x0, local copies, waits for them, and re-layouts: 53.5 us -> none  [the longest x8 53.5 us: toeplitz_rows(): tiled = jnp.tile(flipped, (1, rows + 1))[:, :rows * (length + 1)]]
    rev x4 -> x0, local copies, waits for them, and re-layouts: 47.6 us -> none  [toeplitz_rows(): return jnp.flip(sliding, axis=1)]
    pallas_call x0 -> x1, Pallas kernels: none -> 44.5 us  [body(): pl.pallas_call(kernel_body, out_shape=jax.ShapeDtypeStruct(flat.shape, F3...]
    reshape x6 -> x0, local copies, waits for them, and re-layouts: 42.7 us -> none  [the longest x4 38.8 us: toeplitz_rows(): sliding = tiled.reshape(window.shape[0], rows, length + 1)[:, :, :cols]]
    dot_general x4 -> x0, matrix products: 41.4 us -> none  [one_group(): jnp.einsum('ijk,fxki->fxji', circulant, piece_part, precision=lax.Precisi...]
    ppermute x17 -> x0, starting transfers between devices: 37.3 us -> none  [shifted(): return lax.ppermute(block, axis, route)]
  transfers between devices with their start and end apart: 18 -> 0, of which waited for: 13 -> 0; matrix products, arithmetic and copies ran while one was open for 3% -> 0% of each run, Pallas kernels for 0% -> 0%
where the time goes in v1:
time: 52 us; the launch traced here: 51.7 us
  Pallas kernels  44.5 us (86%)
  local copies, waits for them, and re-layouts  7.22 us (14%)
    pallas_call x1, Pallas kernels, body(): pl.pallas_call(kernel_body, out_shape=jax.ShapeDtypeStruct(flat.shape, F3...  44.5 us
    unnamed x7, local copies, waits for them, and re-layouts  7.22 us

profile of v1, /device:TPU:1, one launch (start us, length us, event | category | flops | bytes accessed | tf_op | source)
XLA Modules:
  0.0 51.7 jit_solution(10793085084162307755)
XLA Ops:
  0.0 0.0 copy-start
  0.0 1.6 %copy-done = bf16[4,512,512]{2,1,0:T(8,128)(2,1)S(1)} copy-done((bf16[4,512,512]{2,1,0:T(8,128)(2,1)S(1)}, bf16[4,512,512]{2,1,0:T(8,128)(2,1)}, u32[]{:S(2)}) %copy-start) | copy-done | bytes 2097176
  1.6 0.0 copy-start.1
  1.6 0.9 %copy-done.1 = f32[64,512]{1,0:T(8,128)S(1)} copy-done((f32[64,512]{1,0:T(8,128)S(1)}, f32[64,512]{1,0:T(8,128)}, u32[]{:S(2)}) %copy-start.1) | copy-done | bytes 131096
  2.5 0.0 copy-start.2
  2.5 0.7 %copy-done.2 = f32[16,64]{1,0:T(8,128)S(1)} copy-done((f32[16,64]{1,0:T(8,128)S(1)}, f32[16,64]{1,0:T(8,128)}, u32[]{:S(2)}) %copy-start.2) | copy-done | bytes 4120
  3.2 44.5 %shard_map.55 = f32[3,512,512]{2,1,0:T(8,128)} custom-call(f32[3,512,512]{2,1,0:T(8,128)} %bitcast.3, f32[64,512]{1,0:T(8,128)S(1)} %copy-done.1, f32[16,64]{1,0:T(8,128)S(1)} %copy-done.2, bf16[4,512,512]{2,1,0:T(8,128)(2,1)S(1)} %copy-done, bf16[2,512,1024]{2,1,0:T(8,128)(2,1)} %constant.5.clone.idft), custom_call_target="tpu_custom_call" | custom-call | tf_op jit(solution)/shard_map/pallas_call | solution.py:559
  47.7 4.0 %copy.7 = f32[3,8,64,512]{3,2,1,0:T(8,128)} copy(f32[3,8,64,512]{3,2,1,0:T(8,128)} %bitcast.2) | data formatting | bytes 6291456
Async XLA Ops:
  0.0 1.6 %copy-start = (bf16[4,512,512]{2,1,0:T(8,128)(2,1)S(1)}, bf16[4,512,512]{2,1,0:T(8,128)(2,1)}, u32[]{:S(2)}) copy-start(bf16[4,512,512]{2,1,0:T(8,128)(2,1)} %constant.4.clone.dft) | copy-start | bytes 6291460
  1.6 0.9 %copy-start.1 = (f32[64,512]{1,0:T(8,128)S(1)}, f32[64,512]{1,0:T(8,128)}, u32[]{:S(2)}) copy-start(f32[64,512]{1,0:T(8,128)} %conduct.1) | copy-start | bytes 393220
  2.5 0.7 %copy-start.2 = (f32[16,64]{1,0:T(8,128)S(1)}, f32[16,64]{1,0:T(8,128)}, u32[]{:S(2)}) copy-start(f32[16,64]{1,0:T(8,128)} %kernel.1) | copy-start | bytes 12292

commit v2 on v1

v2 whole, which is shorter than its diff:
```python
import functools

import jax
import jax.numpy as jnp
import numpy as np
from jax import lax
from jax.experimental import pallas as pl
from jax.experimental.pallas import tpu as pltpu
from jax.sharding import PartitionSpec as P

MESH = pl.DeviceIdType.MESH
F32 = jnp.float32
BF16 = jnp.bfloat16

NF = 3
NX = 8
NB = 64
NQ = 16
HALF = NB * NQ // 2
NEAR = 128
FAR_TILES = 3
FAR = NF * FAR_TILES
MEMBERS = 4
SLICES = NQ // MEMBERS
SLOTS = 3
NEAR_STEPS = (1, 2, 4, 8)
FAR_STEPS = (1, 2)


def transforms():
    points = 2 * HALF
    j = np.arange(HALF)
    forward, inverse = [], []
    for odd in (0, 1):
        freq = 2 * np.arange(HALF // 2) + odd
        angle = 2.0 * np.pi * ((freq[:, None] * j[None, :]) % points) / points
        real, imag = np.cos(angle), -np.sin(angle)
        scale = np.full((HALF // 2, 1), 2.0 / points)
        real_back, imag_back = real * scale, imag * scale
        if not odd:
            imag[0] = np.cos(np.pi * j)
            real_back[0] = 1.0 / points
            imag_back[0] = imag[0] / points
        forward.append(np.concatenate([real, imag]))
        inverse.append(np.concatenate([real_back, imag_back]))
    order = (NB * np.arange(8)[None, :] + np.arange(NB)[:, None]).reshape(-1)
    back = np.concatenate(inverse, axis=0).T[order]
    return np.stack(forward).astype(np.float32), back.astype(np.float32)


def split(x):
    high = x.astype(BF16)
    return high, (x - high.astype(F32)).astype(BF16)


def forward_transform(dft_ref, which, rows):
    high, low = split(rows)
    both = jnp.concatenate([high, low], axis=0)
    contract = (((1,), (1,)), ((), ()))
    one = lax.dot_general(dft_ref[2 * which], both, contract, preferred_element_type=F32)
    two = lax.dot_general(dft_ref[2 * which + 1], high, contract, preferred_element_type=F32)
    return one[:, :128] + one[:, 128:] + two


def inverse_transform(idft_ref, spectrum):
    high, low = split(spectrum)
    both = jnp.concatenate([high, low], axis=1)
    contract = (((1,), (0,)), ((), ()))
    one = lax.dot_general(idft_ref[0], both, contract, preferred_element_type=F32)
    two = lax.dot_general(idft_ref[1], high, contract, preferred_element_type=F32)
    return one[:, :128] + one[:, 128:] + two


def place(count):
    return NB - 2 * count


def coefficients(links, excess, onward, store):
    while links.shape[0] > 1:
        count = links.shape[0] // 2
        pairs = links.reshape(count, 2, 8, 128)
        behind, ahead = pairs[:, 0], pairs[:, 1]
        own = excess.reshape(count, 2, 8, 128)
        inv = 1.0 / (behind + ahead + own[:, 1])
        alpha, beta = behind * inv, ahead * inv
        store(place(count), alpha, beta, inv)
        to_left, to_right = alpha * own[:, 1], beta * own[:, 1]
        excess = own[:, 0] + to_left
        if count > 1:
            excess = jnp.concatenate([excess[:1], excess[1:] + to_right[:-1]], axis=0)
        onward = to_right[count - 1] if onward is None else onward + to_right[count - 1]
        links = behind * beta
    return links[0], excess[0], onward


def reduce_block(values, onward, load, keep):
    while values.shape[0] > 1:
        count = values.shape[0] // 2
        pairs = values.reshape(count, 2, 8, 128)
        even, odd = pairs[:, 0], pairs[:, 1]
        keep(place(count), odd)
        alpha, beta, _ = load(place(count), count)
        to_right = beta * odd
        values = even + alpha * odd
        if count > 1:
            values = jnp.concatenate([values[:1], values[1:] + to_right[:-1]], axis=0)
        onward = to_right[count - 1] if onward is None else onward + to_right[count - 1]
    return values[0], onward


def expand_block(first, following, length, load, kept):
    solved = first[None]
    while solved.shape[0] < length:
        count = solved.shape[0]
        alpha, beta, inv = load(place(count), count)
        right = following[None]
        if count > 1:
            right = jnp.concatenate([solved[1:], right], axis=0)
        odd = inv * kept(place(count), count) + alpha * solved + beta * right
        solved = jnp.stack([solved, odd], axis=1).reshape(2 * count, 8, 128)
    return solved


def ring_coefficients(link, first, onward, steps, prev, ahead):
    excess = first + prev(onward, 1)
    after, before = link, prev(link, 1)
    levels = []
    for d in steps:
        inv = 1.0 / (excess + before + after)
        alpha, beta = before * prev(inv, d), after * ahead(inv, d)
        levels.append((alpha, beta))
        excess = excess + alpha * prev(excess, d) + beta * ahead(excess, d)
        if d < steps[-1]:
            before, after = alpha * prev(before, d), beta * ahead(after, d)
    return levels, 1.0 / excess


def ring_solve(first, onward, levels, final, steps, prev, ahead):
    value = first + prev(onward, 1)
    for d, (alpha, beta) in zip(steps, levels):
        value = value + alpha * prev(value, d) + beta * ahead(value, d)
    return value * final


def far_prev(v, d):
    return jnp.concatenate([v[-d:], v[:-d]], axis=0)


def far_ahead(v, d):
    return jnp.concatenate([v[d:], v[:d]], axis=0)


def near_prev(v, d):
    if d == 8:
        return pltpu.roll(v, 64, 1)
    rolled = pltpu.roll(v, d, 0)
    row = lax.broadcasted_iota(jnp.int32, (8, 128), 0)
    return jnp.where(row >= d, rolled, pltpu.roll(rolled, 64, 1))


def near_ahead(v, d):
    if d == 8:
        return pltpu.roll(v, 64, 1)
    rolled = pltpu.roll(v, 8 - d, 0)
    row = lax.broadcasted_iota(jnp.int32, (8, 128), 0)
    return jnp.where(row < 8 - d, rolled, pltpu.roll(rolled, 64, 1))


def swap_halves(x):
    return pltpu.roll(x, 64, x.ndim - 1)


def each(count, step):
    def run(i, carry):
        step(i)
        return carry

    lax.fori_loop(0, count, run, 0)


def offset(i):
    n = i + 1
    return 8 * lax.rem(n, 2) + 4 * lax.rem(n // 2, 2) + 2 * lax.rem(n // 4, 2) + n // 8


def kernel_body(
    fields, conduct_hbm, kernel_hbm, dft, idft, out,
    held, conduct, kernel, dft_raw, idft_raw, dft_v, idft_v, near_send, near_recv, back_send, back_recv,
    kernel_all, links_send, links_recv, link_rows, rows_ref, freq_ref, spectrum,
    alpha_ref, beta_ref, inv_ref, ring_ref, odd_ref, work,
    far_send, far_recv, slice_send, slice_recv, ring_values, sep_send, sep_recv,
    load_sem, const_sem, ns, nr, bs, br, ks, kr, cs, cr, fs, fr, xs, xr, ss, sr,
):
    me = lax.axis_index("az")
    mx = lax.axis_index("ax")
    ax_count = lax.axis_size("ax")
    member, section = lax.rem(me, MEMBERS), me // MEMBERS
    others = NQ - 1

    def peer(k):
        return lax.rem(me + k, NQ)

    def plane(k):
        return lax.rem(mx + k, ax_count)

    def mate(k):
        return lax.rem(member + k, MEMBERS)

    def remote(src, dst, send, recv, az, ax):
        return pltpu.make_async_remote_copy(
            src, dst, send, recv, device_id={"az": az, "ax": ax}, device_id_type=MESH
        )

    barrier = pltpu.get_barrier_semaphore()

    @functools.partial(each, others)
    def _(i):
        pl.semaphore_signal(barrier, inc=1, device_id={"az": peer(offset(i)), "ax": mx}, device_id_type=MESH)

    @functools.partial(each, ax_count - 1)
    def _(i):
        pl.semaphore_signal(barrier, inc=1, device_id={"az": me, "ax": plane(i + 1)}, device_id_type=MESH)

    def load(f, tile):
        return pltpu.make_async_copy(
            fields.at[f, :, pl.ds(pl.multiple_of(128 * tile, 128), 128)], held.at[f * 4 + tile], load_sem.at[f * 4 + tile]
        )

    small_loads = [
        pltpu.make_async_copy(kernel_hbm, kernel, const_sem.at[2]),
        pltpu.make_async_copy(conduct_hbm, conduct, const_sem.at[3]),
    ]
    const_loads = [
        pltpu.make_async_copy(dft, dft_raw, const_sem.at[0]),
        pltpu.make_async_copy(idft, idft_raw, const_sem.at[1]),
    ]
    each(NF, lambda f: load(f, 0).start())
    for copy in small_loads:
        copy.start()
    each(NF * FAR_TILES, lambda i: load(i // FAR_TILES, lax.rem(i, FAR_TILES) + 1).start())
    for copy in const_loads:
        copy.start()

    def transpose_near(f):
        load(f, 0).wait()

        @functools.partial(each, 4)
        def _(k):
            part = held[f * 4, pl.ds(pl.multiple_of(128 * k, 128), 128), :]
            near_send[f, :, k] = part.T.reshape(NQ, 8, 128)

        near_recv[f, me] = near_send[f, me]

    transpose_near(0)
    for copy in small_loads:
        copy.wait()
    kernel_all[mx] = jnp.concatenate([kernel[0:8, :], kernel[8:16, :]], axis=1)

    pl.semaphore_wait(barrier, others + ax_count - 1)

    @functools.partial(each, ax_count - 1)
    def _(i):
        remote(kernel_all.at[mx], kernel_all.at[mx], ks, kr, me, plane(i + 1)).start()

    kernel_whole = kernel_all.at[pl.ds(0, ax_count - 1)]
    kernel_wait = remote(kernel_whole, kernel_whole, ks, kr, me, plane(1))

    def send_near(f):
        @functools.partial(each, others)
        def _(i):
            k = peer(offset(i))
            remote(near_send.at[f, k], near_recv.at[f, me], ns.at[f], nr.at[f], k, mx).start()

    def near_wait(f):
        whole = pl.ds(0, others)
        return remote(near_send.at[f, whole], near_recv.at[f, whole], ns.at[f], nr.at[f], peer(1), mx)

    send_near(0)

    row = lax.broadcasted_iota(jnp.int32, (8, 128), 0)
    lane = lax.broadcasted_iota(jnp.int32, (8, 128), 1)
    near_links = conduct[:, :NEAR]
    near_links = jnp.concatenate([near_links, near_links], axis=0).T.reshape(NQ, 8, 128)
    kernel_wait.wait_recv()
    kernels = kernel_all[...]
    swapped = swap_halves(kernels.reshape(64, 128)).reshape(8, 8, 128)
    kernels = jnp.stack([swapped, kernels], axis=1).reshape(NQ, 8, 128)
    links_send[...] = jnp.where(lane[None] < 64, near_links, kernels)
    links_recv[me] = links_send[me]

    @functools.partial(each, others)
    def _(i):
        k = peer(offset(i))
        remote(links_send.at[k], links_recv.at[me], cs, cr, k, mx).start()

    links_wait = remote(links_send.at[pl.ds(0, others)], links_recv.at[pl.ds(0, others)], cs, cr, peer(1), mx)
    transpose_near(1)
    send_near(1)
    transpose_near(2)

    def coefficient_store(c):
        def store(offset, alpha, beta, inv):
            count = alpha.shape[0]
            alpha_ref[c, offset : offset + count] = alpha
            beta_ref[c, offset : offset + count] = beta
            inv_ref[c, offset : offset + count] = inv

        return store

    def coefficient_load(c):
        def load(offset, count):
            return (
                alpha_ref[c, offset : offset + count],
                beta_ref[c, offset : offset + count],
                inv_ref[c, offset : offset + count],
            )

        return load

    def odd_keep(w):
        def keep(offset, value):
            odd_ref[w, offset : offset + value.shape[0]] = value

        return keep

    def odd_load(w):
        return lambda offset, count: odd_ref[w, offset : offset + count]

    unit = jnp.ones((NB, 8, 128), F32)

    def packed(link, first, onward):
        return jnp.where(row == 0, link, jnp.where(row == 1, first, onward))

    @functools.partial(each, FAR_TILES)
    def _(lt):
        lanes = pl.ds(pl.multiple_of(128 * lt + NEAR, 128), 128)
        links = jnp.stack([jnp.broadcast_to(conduct[j : j + 1, lanes], (8, 128)) for j in range(NB)])
        tile = packed(*coefficients(links, unit, None, coefficient_store(lt + 1)))
        for f in range(NF):
            far_send[f * FAR_TILES + lt, 2] = tile

    each(NF * FAR_TILES, lambda i: load(i // FAR_TILES, lax.rem(i, FAR_TILES) + 1).wait())

    @functools.partial(each, FAR)
    def _(w):
        f, lt = w // FAR_TILES, lax.rem(w, FAR_TILES)
        values = jnp.stack([held[f * 4 + lt + 1, pl.ds(j, 8, stride=NB), :] for j in range(NB)])
        first, onward = reduce_block(values, None, coefficient_load(lt + 1), odd_keep(w))
        far_send[w, 0] = first
        far_send[w, 1] = onward

    @functools.partial(each, FAR)
    def _(w):
        slot, owner = w // MEMBERS, lax.rem(w, MEMBERS)

        @pl.when(member == owner)
        def _():
            far_recv[slot, member] = far_send[w]

        @pl.when(member != owner)
        def _():
            remote(
                far_send.at[w], far_recv.at[slot, member], fs.at[slot], fr.at[slot], MEMBERS * section + owner, mx
            ).start()

    def far_wait(slot, count):
        return remote(
            far_send.at[pl.ds(0, count)], far_recv.at[slot, pl.ds(0, count)], fs.at[slot], fr.at[slot],
            MEMBERS * section + mate(1), mx,
        )

    send_near(2)

    def far_section(slot):
        far_wait(slot, MEMBERS - 1).wait_recv()
        shape = (MEMBERS, 8, 128)
        link, first, onward = [jnp.broadcast_to(far_recv[slot, :, 2, i : i + 1, :], shape) for i in range(3)]
        first = jnp.concatenate([first[:1], first[1:] + onward[:-1]], axis=0)
        tile = packed(*coefficients(link, first, onward[MEMBERS - 1], coefficient_store(4 + slot)))
        values, onward = far_recv[slot, :, 0], far_recv[slot, :, 1]
        values = jnp.concatenate([values[:1], values[1:] + onward[:-1]], axis=0)
        value, onward = reduce_block(values, onward[MEMBERS - 1], coefficient_load(4 + slot), odd_keep(FAR + 1 + slot))
        slice_send[slot, 0] = value
        slice_send[slot, 1] = onward
        slice_send[slot, 2] = tile
        slice_recv[slot, section] = slice_send[slot]
        for k in range(1, SLICES):
            remote(
                slice_send.at[slot], slice_recv.at[slot, section], xs.at[slot], xr.at[slot], peer(MEMBERS * k), mx
            ).start()

    def slice_wait(slot, sending):
        part = pl.ds(0, SLICES - 1)
        return remote(slice_recv.at[slot, part], slice_recv.at[slot, part], xs.at[slot], xr.at[slot], peer(MEMBERS), mx)

    def far_ring(slot):
        slice_wait(slot, False).wait_recv()
        spread = [jnp.broadcast_to(slice_recv[slot, :, 2, i : i + 1, :], (SLICES, 8, 128)) for i in range(3)]
        levels, final = ring_coefficients(*spread, FAR_STEPS, far_prev, far_ahead)
        value = ring_solve(slice_recv[slot, :, 0], slice_recv[slot, :, 1], levels, final, FAR_STEPS, far_prev, far_ahead)
        ring_values[slot, 0] = value
        ring_values[slot, 1] = far_ahead(value, 1)
        following = ring_values[slot, 1, section]
        solved = expand_block(
            ring_values[slot, 0, section], following, MEMBERS, coefficient_load(4 + slot), odd_load(FAR + 1 + slot)
        )
        sep_send[slot, :, 0] = solved
        sep_send[slot, :, 1] = jnp.concatenate([solved[1:], following[None]], axis=0)
        sep_recv[MEMBERS * slot + member] = sep_send[slot, member]
        for k in range(1, MEMBERS):
            remote(
                sep_send.at[slot, mate(k)], sep_recv.at[MEMBERS * slot + member], ss.at[slot], sr.at[slot],
                MEMBERS * section + mate(k), mx,
            ).start()

    def sep_wait(slot, count):
        return remote(
            sep_send.at[slot, pl.ds(0, count)], sep_recv.at[pl.ds(0, count)], ss.at[slot], sr.at[slot],
            MEMBERS * section + mate(1), mx,
        )

    def each_slot(step):
        @functools.partial(each, SLOTS)
        def _(slot):
            pl.when(MEMBERS * slot + member < FAR)(lambda: step(slot))

    def send_back(f):
        @functools.partial(each, others)
        def _(i):
            k = peer(offset(i))
            remote(back_send.at[f, k], back_recv.at[f, me], bs.at[f], br.at[f], k, mx).start()

    def back_wait(f):
        whole = pl.ds(0, others)
        return remote(back_send.at[f, whole], back_recv.at[f, whole], bs.at[f], br.at[f], peer(1), mx)

    def lay_rows(points, sign):
        total, difference = points[:4] + points[4:], points[:4] - points[4:]
        total = jnp.concatenate([total[m] for m in range(4)], axis=1)
        difference = jnp.concatenate([difference[m] for m in range(4)], axis=1)
        rows_ref[0, 0:64] = total
        rows_ref[0, 64:128] = total
        rows_ref[1, 0:64] = difference
        rows_ref[1, 64:128] = sign * difference

    def kernel_rows():
        links_wait.wait_recv()
        for copy in const_loads:
            copy.wait()
        for odd in range(2):
            dft_v[2 * odd], dft_v[2 * odd + 1] = split(dft_raw[odd])
        idft_v[0], idft_v[1] = split(idft_raw[...])
        pieces = links_recv[...].reshape(8, 2, 8, 128)
        lags = jnp.where(lane[None] < 64, swap_halves(pieces[:, 0].reshape(64, 128)).reshape(8, 8, 128), pieces[:, 1])
        lay_rows(jnp.concatenate([lags] * 8, axis=1), 1.0)

    def kernel_spectrum():
        first_row = lax.broadcasted_iota(jnp.int32, (256, 128), 0) == 0
        real, imag = freq_ref[0, 0:256], freq_ref[0, 256:512]
        spectrum[0] = real
        spectrum[1] = jnp.where(first_row, 0.0, imag)
        spectrum[2] = jnp.where(first_row, imag, real)
        spectrum[3] = freq_ref[1, 0:256]
        spectrum[4] = freq_ref[1, 256:512]

    def near_coefficients():
        @functools.partial(each, 8)
        def _(s):
            rows = jnp.concatenate([links_recv[s]] * 8 + [links_recv[8 + s]] * 8, axis=0)
            link_rows[pl.ds(s, NB, stride=8), :] = rows.T[:NB]

        reduced = coefficients(link_rows[...].reshape(NB, 8, 128), unit, None, coefficient_store(0))
        levels, final = ring_coefficients(*reduced, NEAR_STEPS, near_prev, near_ahead)
        for index, (alpha, beta) in enumerate(levels):
            ring_ref[2 * index] = alpha
            ring_ref[2 * index + 1] = beta
        ring_ref[8] = final

    def near_rows(f):
        near_wait(f).wait_recv()
        pieces = near_recv[f].reshape(8, 2, 4, 8, 128)
        low, high = pieces[:, 0].reshape(256, 128), pieces[:, 1].reshape(256, 128)
        left = lax.broadcasted_iota(jnp.int32, (256, 128), 1) < 64
        plane_a = jnp.where(left, low, swap_halves(high)).reshape(8, 4, 8, 128)
        plane_b = jnp.where(left, swap_halves(low), high).reshape(8, 4, 8, 128)
        lay_rows(jnp.stack([plane_a, plane_b], axis=2).reshape(8, 64, 128), -1.0)

    def near_solve(f):
        real, imag = freq_ref[0, 0:256], freq_ref[0, 256:512]
        odd_real, odd_imag = freq_ref[1, 0:256], freq_ref[1, 256:512]
        product = jnp.concatenate(
            [
                real * spectrum[0] - imag * spectrum[1],
                real * spectrum[1] + imag * spectrum[2],
                odd_real * spectrum[3] - odd_imag * spectrum[4],
                odd_real * spectrum[4] + odd_imag * spectrum[3],
            ],
            axis=0,
        )
        filtered = inverse_transform(idft_v, product).reshape(NB, 8, 128)
        first, onward = reduce_block(filtered, None, coefficient_load(0), odd_keep(FAR))
        ring = [(ring_ref[2 * i], ring_ref[2 * i + 1]) for i in range(4)]
        first = ring_solve(first, onward, ring, ring_ref[8], NEAR_STEPS, near_prev, near_ahead)
        solved = expand_block(first, near_ahead(first, 1), NB, coefficient_load(0), odd_load(FAR))
        work[...] = solved.reshape(512, 128)

        @functools.partial(each, 8)
        def _(s):
            part = work[pl.ds(s, NB, stride=8), :]
            tiles = jnp.concatenate([part, pltpu.roll(part, 120, 1)], axis=0).T
            tiles = tiles.reshape(2, 4, 2, 8, 128)[:, :, 0]
            back_send[f, s] = tiles[0]
            back_send[f, 8 + s] = tiles[1]

        back_recv[f, me] = back_send[f, me]
        send_back(f)

    @functools.partial(each, NF + 1)
    def _(step):
        pl.when(step == 0)(kernel_rows)
        pl.when(step > 0)(lambda: near_rows(step - 1))

        @functools.partial(each, 2)
        def _(odd):
            freq_ref[odd] = forward_transform(dft_v, odd, rows_ref[odd])

        @pl.when(step == 0)
        def _():
            kernel_spectrum()
            near_coefficients()

        pl.when(step > 0)(lambda: near_solve(step - 1))
        pl.when(step == 1)(lambda: each_slot(far_section))
        pl.when(step == 2)(lambda: each_slot(far_ring))

    for slot in range(2):
        sep_wait(slot, MEMBERS - 1).wait_recv()
    pl.when(member != 0)(lambda: sep_wait(2, 1).wait_recv())

    @functools.partial(each, FAR)
    def _(w):
        f, lt = w // FAR_TILES, lax.rem(w, FAR_TILES)
        lanes = pl.ds(pl.multiple_of(128 * lt + NEAR, 128), 128)
        solved = expand_block(sep_recv[w, 0], sep_recv[w, 1], NB, coefficient_load(lt + 1), odd_load(w))
        for j in range(NB):
            work[pl.ds(j, 8, stride=NB), :] = solved[j]
        out[f, :, lanes] = work[...]

    kernel_wait.wait_send()
    links_wait.wait_send()
    each(NF, lambda f: near_wait(f).wait_send())
    for slot in range(2):
        far_wait(slot, MEMBERS - 1).wait_send()
    pl.when(member != 0)(lambda: far_wait(2, 1).wait_send())

    @each_slot
    def _(slot):
        slice_wait(slot, True).wait_send()
        sep_wait(slot, MEMBERS - 1).wait_send()

    @functools.partial(each, NF)
    def _(f):
        back_wait(f).wait_recv()

        @functools.partial(each, 4)
        def _(k):
            tile = back_recv[f, :, k].reshape(128, 128).T
            out[f, pl.ds(pl.multiple_of(128 * k, 128), 128), 0:NEAR] = tile

    each(NF, lambda f: back_wait(f).wait_send())


def body(fields, conduct, kernel):
    dft, idft = transforms()
    shape = fields.shape
    flat = fields.reshape(NF, NX * NB, shape[3])
    vmem = pltpu.VMEM
    dma = pltpu.SemaphoreType.DMA
    anywhere = pl.BlockSpec(memory_space=pl.ANY)
    inside = pl.BlockSpec(memory_space=pltpu.VMEM)
    ax_count = lax.axis_size("ax")
    out = pl.pallas_call(
        kernel_body,
        out_shape=vmem(flat.shape, F32),
        in_specs=[anywhere] * 5,
        out_specs=inside,
        scratch_shapes=[
            vmem((12, 512, 128), F32),
            vmem(conduct.shape, F32),
            vmem(kernel.shape, F32),
            vmem((2, 512, 512), F32),
            vmem((512, 1024), F32),
            vmem((4, 512, 512), BF16),
            vmem((2, 512, 1024), BF16),
            vmem((NF, NQ, 4, 8, 128), F32),
            vmem((NF, NQ, 4, 8, 128), F32),
            vmem((NF, NQ, 4, 8, 128), F32),
            vmem((NF, NQ, 4, 8, 128), F32),
            vmem((ax_count, 8, 128), F32),
            vmem((NQ, 8, 128), F32),
            vmem((NQ, 8, 128), F32),
            vmem((512, 128), F32),
            vmem((2, 128, 512), F32),
            vmem((2, 512, 128), F32),
            vmem((5, 256, 128), F32),
            vmem((4 + SLOTS, NB, 8, 128), F32),
            vmem((4 + SLOTS, NB, 8, 128), F32),
            vmem((4 + SLOTS, NB, 8, 128), F32),
            vmem((9, 8, 128), F32),
            vmem((FAR + 1 + SLOTS, NB, 8, 128), F32),
            vmem((512, 128), F32),
            vmem((FAR, 3, 8, 128), F32),
            vmem((SLOTS, MEMBERS, 3, 8, 128), F32),
            vmem((SLOTS, 3, 8, 128), F32),
            vmem((SLOTS, SLICES, 3, 8, 128), F32),
            vmem((SLOTS, 2, SLICES, 8, 128), F32),
            vmem((SLOTS, MEMBERS, 2, 8, 128), F32),
            vmem((FAR, 2, 8, 128), F32),
            dma((12,)), dma((4,)),
            dma((NF,)), dma((NF,)), dma((NF,)), dma((NF,)),
            dma, dma, dma, dma,
            dma((SLOTS,)), dma((SLOTS,)), dma((SLOTS,)), dma((SLOTS,)), dma((SLOTS,)), dma((SLOTS,)),
        ],
        compiler_params=pltpu.CompilerParams(
            collective_id=0, has_side_effects=True, vmem_limit_bytes=int(60.9 * 2**20)
        ),
    )(flat, conduct, kernel, jnp.asarray(dft), jnp.asarray(idft))
    return out.reshape(shape)


def solution(mesh):
    return jax.shard_map(
        body,
        mesh=mesh,
        in_specs=(P(None, "ax", "az", None), P("az", None), P("ax", "az")),
        out_specs=P(None, "ax", "az", None),
        check_vma=False,
    )
```

time: 52 us -> 41.6 us (0.80)
  local copies, waits for them, and re-layouts: 7.22 us -> 1.67 us
  Pallas kernels: 44.5 us -> 39.8 us
    unnamed x7 -> x1, local copies, waits for them, and re-layouts: 7.22 us -> 1.67 us
    pallas_call x1, Pallas kernels: 44.5 us -> 39.8 us  [body(): pl.pallas_call(kernel_body, out_shape=vmem(flat.shape, F32), in_specs=[an...]
where the time goes in v2:
time: 41.6 us; the launch traced here: 41.5 us
  Pallas kernels  39.8 us (96%)
  local copies, waits for them, and re-layouts  1.67 us (4%)
    pallas_call x1, Pallas kernels, body(): pl.pallas_call(kernel_body, out_shape=vmem(flat.shape, F32), in_specs=[an...  39.8 us
    unnamed x1, local copies, waits for them, and re-layouts  1.67 us

profile of v2, /device:TPU:1, one launch (start us, length us, event | category | flops | bytes accessed | tf_op | source)
XLA Modules:
  0.0 41.5 jit_solution(5629815255468676300)
XLA Ops:
  0.0 39.8 %shard_map.55 = f32[3,512,512]{2,1,0:T(8,128)S(1)} custom-call(f32[3,512,512]{2,1,0:T(8,128)} %bitcast.3, f32[64,512]{1,0:T(8,128)} %conduct_hbm.1, f32[16,64]{1,0:T(8,128)} %kernel_hbm.1, f32[2,512,512]{2,1,0:T(8,128)} %constant.4.clone.dft, f32[512,1024]{1,0:T(8,128)} %constant.5.clone.idft), custom_call_target="tpu_custom_call" | custom-call | tf_op jit(solution)/shard_map/pallas_call | solution.py:582
  39.8 1.7 %copy.7 = f32[3,8,64,512]{3,2,1,0:T(8,128)} copy(f32[3,8,64,512]{3,2,1,0:T(8,128)S(1)} %bitcast.2) | data formatting | bytes 6291456

commit v3 on v2

--- a/solution.py
+++ b/solution.py
@@ -25,6 +25,7 @@
 SLOTS = 3
 NEAR_STEPS = (1, 2, 4, 8)
 FAR_STEPS = (1, 2)
+ORDER = (8, 4, 12, 1, 9, 5, 13, 2, 10, 6, 14, 3, 11, 7, 15)
 
 
 def transforms():
@@ -150,20 +151,26 @@
     return jnp.concatenate([v[d:], v[:d]], axis=0)
 
 
+def twin(v):
+    return jnp.stack([v, pltpu.roll(v, 64, 1)])
+
+
+def near_shift(v, d, ahead):
+    if d == 8:
+        return jnp.stack([v[1], v[0]])
+    row = lax.broadcasted_iota(jnp.int32, (8, 128), 0)
+    inside = row < 8 - d if ahead else row >= d
+    turn = 8 - d if ahead else d
+    one, two = pltpu.roll(v[0], turn, 0), pltpu.roll(v[1], turn, 0)
+    return jnp.stack([jnp.where(inside, one, two), jnp.where(inside, two, one)])
+
+
 def near_prev(v, d):
-    if d == 8:
-        return pltpu.roll(v, 64, 1)
-    rolled = pltpu.roll(v, d, 0)
-    row = lax.broadcasted_iota(jnp.int32, (8, 128), 0)
-    return jnp.where(row >= d, rolled, pltpu.roll(rolled, 64, 1))
+    return near_shift(v, d, False)
 
 
 def near_ahead(v, d):
-    if d == 8:
-        return pltpu.roll(v, 64, 1)
-    rolled = pltpu.roll(v, 8 - d, 0)
-    row = lax.broadcasted_iota(jnp.int32, (8, 128), 0)
-    return jnp.where(row < 8 - d, rolled, pltpu.roll(rolled, 64, 1))
+    return near_shift(v, d, True)
 
 
 def swap_halves(x):
@@ -178,9 +185,8 @@
     lax.fori_loop(0, count, run, 0)
 
 
-def offset(i):
-    n = i + 1
-    return 8 * lax.rem(n, 2) + 4 * lax.rem(n // 2, 2) + 2 * lax.rem(n // 4, 2) + n // 8
+def wrap(i, count):
+    return jnp.where(i >= count, i - count, i)
 
 
 def kernel_body(
@@ -198,13 +204,13 @@
     others = NQ - 1
 
     def peer(k):
-        return lax.rem(me + k, NQ)
+        return wrap(me + k, NQ)
 
     def plane(k):
-        return lax.rem(mx + k, ax_count)
+        return wrap(mx + k, ax_count)
 
     def mate(k):
-        return lax.rem(member + k, MEMBERS)
+        return wrap(member + k, MEMBERS)
 
     def remote(src, dst, send, recv, az, ax):
         return pltpu.make_async_remote_copy(
@@ -213,13 +219,10 @@
 
     barrier = pltpu.get_barrier_semaphore()
 
-    @functools.partial(each, others)
-    def _(i):
-        pl.semaphore_signal(barrier, inc=1, device_id={"az": peer(offset(i)), "ax": mx}, device_id_type=MESH)
-
-    @functools.partial(each, ax_count - 1)
-    def _(i):
-        pl.semaphore_signal(barrier, inc=1, device_id={"az": me, "ax": plane(i + 1)}, device_id_type=MESH)
+    for k in ORDER:
+        pl.semaphore_signal(barrier, inc=1, device_id={"az": peer(k), "ax": mx}, device_id_type=MESH)
+    for k in range(1, ax_count):
+        pl.semaphore_signal(barrier, inc=1, device_id={"az": me, "ax": plane(k)}, device_id_type=MESH)
 
     def load(f, tile):
         return pltpu.make_async_copy(
@@ -237,7 +240,7 @@
     each(NF, lambda f: load(f, 0).start())
     for copy in small_loads:
         copy.start()
-    each(NF * FAR_TILES, lambda i: load(i // FAR_TILES, lax.rem(i, FAR_TILES) + 1).start())
+    each(NF, lambda f: each(FAR_TILES, lambda lt: load(f, lt + 1).start()))
     for copy in const_loads:
         copy.start()
 
@@ -258,17 +261,12 @@
 
     pl.semaphore_wait(barrier, others + ax_count - 1)
 
-    @functools.partial(each, ax_count - 1)
-    def _(i):
-        remote(kernel_all.at[mx], kernel_all.at[mx], ks, kr, me, plane(i + 1)).start()
 
     kernel_whole = kernel_all.at[pl.ds(0, ax_count - 1)]
     kernel_wait = remote(kernel_whole, kernel_whole, ks, kr, me, plane(1))
 
     def send_near(f):
-        @functools.partial(each, others)
-        def _(i):
-            k = peer(offset(i))
+        for k in map(peer, ORDER):
             remote(near_send.at[f, k], near_recv.at[f, me], ns.at[f], nr.at[f], k, mx).start()
 
     def near_wait(f):
@@ -276,9 +274,84 @@
         return remote(near_send.at[f, whole], near_recv.at[f, whole], ns.at[f], nr.at[f], peer(1), mx)
 
     send_near(0)
-
+    for k in range(1, ax_count):
+        remote(kernel_all.at[mx], kernel_all.at[mx], ks, kr, me, plane(k)).start()
+    transpose_near(1)
+    transpose_near(2)
     row = lax.broadcasted_iota(jnp.int32, (8, 128), 0)
     lane = lax.broadcasted_iota(jnp.int32, (8, 128), 1)
+
+    def coefficient_store(c):
+        def store(offset, alpha, beta, inv):
+            count = alpha.shape[0]
+            alpha_ref[c, offset : offset + count] = alpha
+            beta_ref[c, offset : offset + count] = beta
+            inv_ref[c, offset : offset + count] = inv
+
+        return store
+
+    def coefficient_load(c):
+        def load(offset, count):
+            return (
+                alpha_ref[c, offset : offset + count],
+                beta_ref[c, offset : offset + count],
+                inv_ref[c, offset : offset + count],
+            )
+
+        return load
+
+    def odd_keep(w):
+        def keep(offset, value):
+            odd_ref[w, offset : offset + value.shape[0]] = value
+
+        return keep
+
+    def odd_load(w):
+        return lambda offset, count: odd_ref[w, offset : offset + count]
+
+    unit = jnp.ones((NB, 8, 128), F32)
+
+    def packed(link, first, onward):
+        return jnp.where(row == 0, link, jnp.where(row == 1, first, onward))
+
+    @functools.partial(each, FAR_TILES)
+    def _(lt):
+        lanes = pl.ds(pl.multiple_of(128 * lt + NEAR, 128), 128)
+        links = jnp.stack([jnp.broadcast_to(conduct[j : j + 1, lanes], (8, 128)) for j in range(NB)])
+        tile = packed(*coefficients(links, unit, None, coefficient_store(lt + 1)))
+        for f in range(NF):
+            far_send[f * FAR_TILES + lt, 2] = tile
+
+    each(NF, lambda f: each(FAR_TILES, lambda lt: load(f, lt + 1).wait()))
+
+    def far_reduce(f, lt):
+        w = f * FAR_TILES + lt
+        values = jnp.stack([held[f * 4 + lt + 1, pl.ds(j, 8, stride=NB), :] for j in range(NB)])
+        first, onward = reduce_block(values, None, coefficient_load(lt + 1), odd_keep(w))
+        far_send[w, 0] = first
+        far_send[w, 1] = onward
+
+    each(NF, lambda f: each(FAR_TILES, lambda lt: far_reduce(f, lt)))
+
+    for w in range(FAR):
+        slot, owner = w // MEMBERS, w % MEMBERS
+
+        @pl.when(member == owner)
+        def _():
+            far_recv[slot, member] = far_send[w]
+
+        @pl.when(member != owner)
+        def _():
+            remote(
+                far_send.at[w], far_recv.at[slot, member], fs.at[slot], fr.at[slot], MEMBERS * section + owner, mx
+            ).start()
+
+    def far_wait(slot, count):
+        return remote(
+            far_send.at[pl.ds(0, count)], far_recv.at[slot, pl.ds(0, count)], fs.at[slot], fr.at[slot],
+            MEMBERS * section + mate(1), mx,
+        )
+
     near_links = conduct[:, :NEAR]
     near_links = jnp.concatenate([near_links, near_links], axis=0).T.reshape(NQ, 8, 128)
     kernel_wait.wait_recv()
@@ -288,87 +361,20 @@
     links_send[...] = jnp.where(lane[None] < 64, near_links, kernels)
     links_recv[me] = links_send[me]
 
-    @functools.partial(each, others)
-    def _(i):
-        k = peer(offset(i))
+    for k in map(peer, ORDER):
         remote(links_send.at[k], links_recv.at[me], cs, cr, k, mx).start()
 
     links_wait = remote(links_send.at[pl.ds(0, others)], links_recv.at[pl.ds(0, others)], cs, cr, peer(1), mx)
-    transpose_near(1)
+    near_wait(0).wait_send()
     send_near(1)
-    transpose_near(2)
-
-    def coefficient_store(c):
-        def store(offset, alpha, beta, inv):
-            count = alpha.shape[0]
-            alpha_ref[c, offset : offset + count] = alpha
-            beta_ref[c, offset : offset + count] = beta
-            inv_ref[c, offset : offset + count] = inv
-
-        return store
-
-    def coefficient_load(c):
-        def load(offset, count):
-            return (
-                alpha_ref[c, offset : offset + count],
-                beta_ref[c, offset : offset + count],
-                inv_ref[c, offset : offset + count],
-            )
-
-        return load
-
-    def odd_keep(w):
-        def keep(offset, value):
-            odd_ref[w, offset : offset + value.shape[0]] = value
-
-        return keep
-
-    def odd_load(w):
-        return lambda offset, count: odd_ref[w, offset : offset + count]
-
-    unit = jnp.ones((NB, 8, 128), F32)
-
-    def packed(link, first, onward):
-        return jnp.where(row == 0, link, jnp.where(row == 1, first, onward))
-
-    @functools.partial(each, FAR_TILES)
-    def _(lt):
-        lanes = pl.ds(pl.multiple_of(128 * lt + NEAR, 128), 128)
-        links = jnp.stack([jnp.broadcast_to(conduct[j : j + 1, lanes], (8, 128)) for j in range(NB)])
-        tile = packed(*coefficients(links, unit, None, coefficient_store(lt + 1)))
-        for f in range(NF):
-            far_send[f * FAR_TILES + lt, 2] = tile
-
-    each(NF * FAR_TILES, lambda i: load(i // FAR_TILES, lax.rem(i, FAR_TILES) + 1).wait())
-
-    @functools.partial(each, FAR)
-    def _(w):
-        f, lt = w // FAR_TILES, lax.rem(w, FAR_TILES)
-        values = jnp.stack([held[f * 4 + lt + 1, pl.ds(j, 8, stride=NB), :] for j in range(NB)])
-        first, onward = reduce_block(values, None, coefficient_load(lt + 1), odd_keep(w))
-        far_send[w, 0] = first
-        far_send[w, 1] = onward
-
-    @functools.partial(each, FAR)
-    def _(w):
-        slot, owner = w // MEMBERS, lax.rem(w, MEMBERS)
-
-        @pl.when(member == owner)
-        def _():
-            far_recv[slot, member] = far_send[w]
-
-        @pl.when(member != owner)
-        def _():
-            remote(
-                far_send.at[w], far_recv.at[slot, member], fs.at[slot], fr.at[slot], MEMBERS * section + owner, mx
-            ).start()
-
-    def far_wait(slot, count):
-        return remote(
-            far_send.at[pl.ds(0, count)], far_recv.at[slot, pl.ds(0, count)], fs.at[slot], fr.at[slot],
-            MEMBERS * section + mate(1), mx,
-        )
-
+
+    for copy in const_loads:
+        copy.wait()
+    for odd in range(2):
+        dft_v[2 * odd], dft_v[2 * odd + 1] = split(dft_raw[odd])
+    idft_v[0], idft_v[1] = split(idft_raw[...])
+
+    near_wait(1).wait_send()
     send_near(2)
 
     def far_section(slot):
@@ -425,43 +431,37 @@
             pl.when(MEMBERS * slot + member < FAR)(lambda: step(slot))
 
     def send_back(f):
-        @functools.partial(each, others)
-        def _(i):
-            k = peer(offset(i))
+        for k in map(peer, ORDER):
             remote(back_send.at[f, k], back_recv.at[f, me], bs.at[f], br.at[f], k, mx).start()
 
     def back_wait(f):
         whole = pl.ds(0, others)
         return remote(back_send.at[f, whole], back_recv.at[f, whole], bs.at[f], br.at[f], peer(1), mx)
 
-    def lay_rows(points, sign):
+    def lay_rows(points, place):
         total, difference = points[:4] + points[4:], points[:4] - points[4:]
-        total = jnp.concatenate([total[m] for m in range(4)], axis=1)
-        difference = jnp.concatenate([difference[m] for m in range(4)], axis=1)
-        rows_ref[0, 0:64] = total
-        rows_ref[0, 64:128] = total
-        rows_ref[1, 0:64] = difference
-        rows_ref[1, 64:128] = sign * difference
+        rows_ref[0, place : place + 64] = jnp.concatenate([total[m] for m in range(4)], axis=1)
+        rows_ref[1, place : place + 64] = jnp.concatenate([difference[m] for m in range(4)], axis=1)
 
     def kernel_rows():
-        links_wait.wait_recv()
-        for copy in const_loads:
-            copy.wait()
-        for odd in range(2):
-            dft_v[2 * odd], dft_v[2 * odd + 1] = split(dft_raw[odd])
-        idft_v[0], idft_v[1] = split(idft_raw[...])
         pieces = links_recv[...].reshape(8, 2, 8, 128)
         lags = jnp.where(lane[None] < 64, swap_halves(pieces[:, 0].reshape(64, 128)).reshape(8, 8, 128), pieces[:, 1])
-        lay_rows(jnp.concatenate([lags] * 8, axis=1), 1.0)
+        lay_rows(jnp.concatenate([lags] * 8, axis=1), 64)
+
+    left = lax.broadcasted_iota(jnp.int32, (256, 128), 1) < 64
 
     def kernel_spectrum():
+        def both(odd, half):
+            value = freq_ref[odd, 256 * half : 256 * half + 256]
+            return jnp.where(left, swap_halves(value), value)
+
         first_row = lax.broadcasted_iota(jnp.int32, (256, 128), 0) == 0
-        real, imag = freq_ref[0, 0:256], freq_ref[0, 256:512]
+        real, imag = both(0, 0), both(0, 1)
         spectrum[0] = real
         spectrum[1] = jnp.where(first_row, 0.0, imag)
         spectrum[2] = jnp.where(first_row, imag, real)
-        spectrum[3] = freq_ref[1, 0:256]
-        spectrum[4] = freq_ref[1, 256:512]
+        spectrum[3] = both(1, 0)
+        spectrum[4] = both(1, 1)
 
     def near_coefficients():
         @functools.partial(each, 8)
@@ -470,7 +470,7 @@
             link_rows[pl.ds(s, NB, stride=8), :] = rows.T[:NB]
 
         reduced = coefficients(link_rows[...].reshape(NB, 8, 128), unit, None, coefficient_store(0))
-        levels, final = ring_coefficients(*reduced, NEAR_STEPS, near_prev, near_ahead)
+        levels, final = ring_coefficients(*[twin(v) for v in reduced], NEAR_STEPS, near_prev, near_ahead)
         for index, (alpha, beta) in enumerate(levels):
             ring_ref[2 * index] = alpha
             ring_ref[2 * index + 1] = beta
@@ -480,14 +480,17 @@
         near_wait(f).wait_recv()
         pieces = near_recv[f].reshape(8, 2, 4, 8, 128)
         low, high = pieces[:, 0].reshape(256, 128), pieces[:, 1].reshape(256, 128)
-        left = lax.broadcasted_iota(jnp.int32, (256, 128), 1) < 64
         plane_a = jnp.where(left, low, swap_halves(high)).reshape(8, 4, 8, 128)
         plane_b = jnp.where(left, swap_halves(low), high).reshape(8, 4, 8, 128)
-        lay_rows(jnp.stack([plane_a, plane_b], axis=2).reshape(8, 64, 128), -1.0)
+        lay_rows(jnp.stack([plane_a, plane_b], axis=2).reshape(8, 64, 128), 0)
 
     def near_solve(f):
-        real, imag = freq_ref[0, 0:256], freq_ref[0, 256:512]
-        odd_real, odd_imag = freq_ref[1, 0:256], freq_ref[1, 256:512]
+        def both(odd, half, sign):
+            value = freq_ref[odd, 256 * half : 256 * half + 256]
+            return jnp.where(left, value, sign * swap_halves(value))
+
+        real, imag = both(0, 0, 1.0), both(0, 1, 1.0)
+        odd_real, odd_imag = both(1, 0, -1.0), both(1, 1, -1.0)
         product = jnp.concatenate(
             [
                 real * spectrum[0] - imag * spectrum[1],
@@ -500,8 +503,8 @@
         filtered = inverse_transform(idft_v, product).reshape(NB, 8, 128)
         first, onward = reduce_block(filtered, None, coefficient_load(0), odd_keep(FAR))
         ring = [(ring_ref[2 * i], ring_ref[2 * i + 1]) for i in range(4)]
-        first = ring_solve(first, onward, ring, ring_ref[8], NEAR_STEPS, near_prev, near_ahead)
-        solved = expand_block(first, near_ahead(first, 1), NB, coefficient_load(0), odd_load(FAR))
+        first = ring_solve(twin(first), twin(onward), ring, ring_ref[8], NEAR_STEPS, near_prev, near_ahead)
+        solved = expand_block(first[0], near_ahead(first, 1)[0], NB, coefficient_load(0), odd_load(FAR))
         work[...] = solved.reshape(512, 128)
 
         @functools.partial(each, 8)
@@ -515,40 +518,40 @@
         back_recv[f, me] = back_send[f, me]
         send_back(f)
 
-    @functools.partial(each, NF + 1)
-    def _(step):
-        pl.when(step == 0)(kernel_rows)
-        pl.when(step > 0)(lambda: near_rows(step - 1))
+    links_wait.wait_recv()
+    kernel_rows()
+    near_coefficients()
+    each_slot(far_section)
+
+    @functools.partial(each, NF)
+    def _(f):
+        near_rows(f)
 
         @functools.partial(each, 2)
         def _(odd):
             freq_ref[odd] = forward_transform(dft_v, odd, rows_ref[odd])
 
-        @pl.when(step == 0)
-        def _():
-            kernel_spectrum()
-            near_coefficients()
-
-        pl.when(step > 0)(lambda: near_solve(step - 1))
-        pl.when(step == 1)(lambda: each_slot(far_section))
-        pl.when(step == 2)(lambda: each_slot(far_ring))
+        pl.when(f == 0)(kernel_spectrum)
+        near_solve(f)
+        pl.when(f == 1)(lambda: each_slot(far_ring))
 
     for slot in range(2):
         sep_wait(slot, MEMBERS - 1).wait_recv()
     pl.when(member != 0)(lambda: sep_wait(2, 1).wait_recv())
 
-    @functools.partial(each, FAR)
-    def _(w):
-        f, lt = w // FAR_TILES, lax.rem(w, FAR_TILES)
+    def far_expand(f, lt):
+        w = f * FAR_TILES + lt
         lanes = pl.ds(pl.multiple_of(128 * lt + NEAR, 128), 128)
         solved = expand_block(sep_recv[w, 0], sep_recv[w, 1], NB, coefficient_load(lt + 1), odd_load(w))
         for j in range(NB):
             work[pl.ds(j, 8, stride=NB), :] = solved[j]
         out[f, :, lanes] = work[...]
 
+    each(NF, lambda f: each(FAR_TILES, lambda lt: far_expand(f, lt)))
+
     kernel_wait.wait_send()
     links_wait.wait_send()
-    each(NF, lambda f: near_wait(f).wait_send())
+    near_wait(2).wait_send()
     for slot in range(2):
         far_wait(slot, MEMBERS - 1).wait_send()
     pl.when(member != 0)(lambda: far_wait(2, 1).wait_send())
@@ -606,7 +609,7 @@
             vmem((4 + SLOTS, NB, 8, 128), F32),
             vmem((4 + SLOTS, NB, 8, 128), F32),
             vmem((4 + SLOTS, NB, 8, 128), F32),
-            vmem((9, 8, 128), F32),
+            vmem((9, 2, 8, 128), F32),
             vmem((FAR + 1 + SLOTS, NB, 8, 128), F32),
             vmem((512, 128), F32),
             vmem((FAR, 3, 8, 128), F32),

time: 41.6 us -> 37.7 us (0.906)
  Pallas kernels: 39.8 us -> 35.9 us
    pallas_call x1, Pallas kernels: 39.8 us -> 35.9 us  [body(): pl.pallas_call(kernel_body, out_shape=vmem(flat.shape, F32), in_specs=[an...]
where the time goes in v3:
time: 37.7 us; the launch traced here: 37.6 us
  Pallas kernels  35.9 us (95%)
  local copies, waits for them, and re-layouts  1.67 us (4%)
    pallas_call x1, Pallas kernels, body(): pl.pallas_call(kernel_body, out_shape=vmem(flat.shape, F32), in_specs=[an...  35.9 us
    unnamed x1, local copies, waits for them, and re-layouts  1.67 us

profile of v3, /device:TPU:1, one launch (start us, length us, event | category | flops | bytes accessed | tf_op | source)
XLA Modules:
  0.0 37.6 jit_solution(1359755985929169107)
XLA Ops:
  0.0 35.9 %shard_map.55 = f32[3,512,512]{2,1,0:T(8,128)S(1)} custom-call(f32[3,512,512]{2,1,0:T(8,128)} %bitcast.3, f32[64,512]{1,0:T(8,128)} %conduct_hbm.1, f32[16,64]{1,0:T(8,128)} %kernel_hbm.1, f32[2,512,512]{2,1,0:T(8,128)} %constant.4.clone.dft, f32[512,1024]{1,0:T(8,128)} %constant.5.clone.idft), custom_call_target="tpu_custom_call" | custom-call | tf_op jit(solution)/shard_map/pallas_call | solution.py:585
  36.0 1.7 %copy.7 = f32[3,8,64,512]{3,2,1,0:T(8,128)} copy(f32[3,8,64,512]{3,2,1,0:T(8,128)S(1)} %bitcast.2) | data formatting | bytes 6291456

commit v4 on v3

--- a/solution.py
+++ b/solution.py
@@ -464,8 +464,7 @@
         spectrum[4] = both(1, 1)
 
     def near_coefficients():
-        @functools.partial(each, 8)
-        def _(s):
+        for s in range(8):
             rows = jnp.concatenate([links_recv[s]] * 8 + [links_recv[8 + s]] * 8, axis=0)
             link_rows[pl.ds(s, NB, stride=8), :] = rows.T[:NB]
 
@@ -507,8 +506,7 @@
         solved = expand_block(first[0], near_ahead(first, 1)[0], NB, coefficient_load(0), odd_load(FAR))
         work[...] = solved.reshape(512, 128)
 
-        @functools.partial(each, 8)
-        def _(s):
+        for s in range(8):
             part = work[pl.ds(s, NB, stride=8), :]
             tiles = jnp.concatenate([part, pltpu.roll(part, 120, 1)], axis=0).T
             tiles = tiles.reshape(2, 4, 2, 8, 128)[:, :, 0]
@@ -565,10 +563,8 @@
     def _(f):
         back_wait(f).wait_recv()
 
-        @functools.partial(each, 4)
-        def _(k):
-            tile = back_recv[f, :, k].reshape(128, 128).T
-            out[f, pl.ds(pl.multiple_of(128 * k, 128), 128), 0:NEAR] = tile
+        for k in range(4):
+            out[f, 128 * k : 128 * k + 128, 0:NEAR] = back_recv[f, :, k].reshape(128, 128).T
 
     each(NF, lambda f: back_wait(f).wait_send())
 

time: 37.7 us -> 36.2 us (0.960)
  Pallas kernels: 35.9 us -> 34.4 us
    pallas_call x1, Pallas kernels: 35.9 us -> 34.4 us  [body(): pl.pallas_call(kernel_body, out_shape=vmem(flat.shape, F32), in_specs=[an...]
where the time goes in v4:
time: 36.2 us; the launch traced here: 36.1 us
  Pallas kernels  34.4 us (95%)
  local copies, waits for them, and re-layouts  1.67 us (5%)
    pallas_call x1, Pallas kernels, body(): pl.pallas_call(kernel_body, out_shape=vmem(flat.shape, F32), in_specs=[an...  34.4 us
    unnamed x1, local copies, waits for them, and re-layouts  1.67 us

profile of v4, /device:TPU:1, one launch (start us, length us, event | category | flops | bytes accessed | tf_op | source)
XLA Modules:
  0.0 36.1 jit_solution(12931024329485751894)
XLA Ops:
  0.0 34.4 %shard_map.55 = f32[3,512,512]{2,1,0:T(8,128)S(1)} custom-call(f32[3,512,512]{2,1,0:T(8,128)} %bitcast.3, f32[64,512]{1,0:T(8,128)} %conduct_hbm.1, f32[16,64]{1,0:T(8,128)} %kernel_hbm.1, f32[2,512,512]{2,1,0:T(8,128)} %constant.4.clone.dft, f32[512,1024]{1,0:T(8,128)} %constant.5.clone.idft), custom_call_target="tpu_custom_call" | custom-call | tf_op jit(solution)/shard_map/pallas_call | solution.py:581
  34.4 1.7 %copy.7 = f32[3,8,64,512]{3,2,1,0:T(8,128)} copy(f32[3,8,64,512]{3,2,1,0:T(8,128)S(1)} %bitcast.2) | data formatting | bytes 6291456

commit v5 on v4

--- a/solution.py
+++ b/solution.py
@@ -247,10 +247,8 @@
     def transpose_near(f):
         load(f, 0).wait()
 
-        @functools.partial(each, 4)
-        def _(k):
-            part = held[f * 4, pl.ds(pl.multiple_of(128 * k, 128), 128), :]
-            near_send[f, :, k] = part.T.reshape(NQ, 8, 128)
+        for k in range(4):
+            near_send[f, :, k] = held[f * 4, 128 * k : 128 * k + 128, :].T.reshape(NQ, 8, 128)
 
         near_recv[f, me] = near_send[f, me]
 

time: 36.2 us -> 36.2 us (level)
  no operation moved by 1% of the time
where the time goes in v5:
time: 36.2 us; the launch traced here: 36.1 us
  Pallas kernels  34.4 us (95%)
  local copies, waits for them, and re-layouts  1.67 us (5%)
    pallas_call x1, Pallas kernels, body(): pl.pallas_call(kernel_body, out_shape=vmem(flat.shape, F32), in_specs=[an...  34.4 us
    unnamed x1, local copies, waits for them, and re-layouts  1.67 us

profile of v5, /device:TPU:1, one launch (start us, length us, event | category | flops | bytes accessed | tf_op | source)
XLA Modules:
  0.0 36.1 jit_solution(12866323965646268128)
XLA Ops:
  0.0 34.4 %shard_map.55 = f32[3,512,512]{2,1,0:T(8,128)S(1)} custom-call(f32[3,512,512]{2,1,0:T(8,128)} %bitcast.3, f32[64,512]{1,0:T(8,128)} %conduct_hbm.1, f32[16,64]{1,0:T(8,128)} %kernel_hbm.1, f32[2,512,512]{2,1,0:T(8,128)} %constant.4.clone.dft, f32[512,1024]{1,0:T(8,128)} %constant.5.clone.idft), custom_call_target="tpu_custom_call" | custom-call | tf_op jit(solution)/shard_map/pallas_call | solution.py:579
  34.4 1.7 %copy.7 = f32[3,8,64,512]{3,2,1,0:T(8,128)} copy(f32[3,8,64,512]{3,2,1,0:T(8,128)S(1)} %bitcast.2) | data formatting | bytes 6291456
